TPU v7x, 32 devices: a whole 2x2x4 slice. The times are simulated.
32 devices in a mesh: gx: 4 (over z), gy: 8 (over y, x, core).
Axes of the slice: x: 2, y: 2, z: 4, core: 2. Of those that a mesh axis runs over, the one named last changes fastest.
Arguments:
- populations: float32 [27, 128, 8192], P(None, 'gx', 'gy'), may hold values from 0.002 to 0.42, as said below
- adjoint_in: float32 [27, 128, 8192], P(None, 'gx', 'gy'), may hold values from -6 to 6
- porosity: float32 [128, 8192], P('gx', 'gy'), may hold values from 0.1 to 10
- solid: int32 [128, 8192], P('gx', 'gy'), may hold values 0 or 1
- labels: int32 [128, 8192], P('gx', 'gy'), may hold values from 0 to 2
Outputs:
- final_pops: float32 [27, 128, 8192], P(None, 'gx', 'gy')
- adjoint_out: float32 [27, 128, 8192], P(None, 'gx', 'gy')
- sensitivity: float32 [128, 8192], P('gx', 'gy')
Inputs may be any that keep to these rules, and one draw needn't show every extreme that they name: `populations`: every population is between 0.6 and 1.4 times its weight w_i.
All inputs are finite; a program needn't handle non-finite values. Where the computation divides by a largest or mean magnitude, that divisor is 1e-20 or more. No bound on the sum of `solid` on one device may be relied on, other than what follows from the above.
Results may differ from a plain program's by a relative error of at most 0.0001.
Values sent between devices are 32-bit elements; how exact they have to be, the bound alone decides.
No kernel may reach another device: no remote copies, remote signals or barrier semaphores. Data moves between devices by JAX's collectives and lax.ppermute only.
A program may use at most 128 MiB of HBM per device.

v0:
```python
import jax
import jax.numpy as jnp
from jax import lax
from jax.sharding import PartitionSpec as P

NZ = 64
STEPS = 2


RELAX = 0.8
PUSH = 0.2
EPS = 1e-06
velocity_vectors = [(a, b, c) for a in (-1, 0, 1) for b in (-1, 0, 1) for c in (-1, 0, 1)]
vel_x = [float(v[0]) for v in velocity_vectors]
vel_y = [float(v[1]) for v in velocity_vectors]
vel_z = [float(v[2]) for v in velocity_vectors]
weight_table = [
    [8.0 / 27, 2.0 / 27, 1.0 / 54, 1.0 / 216][abs(v[0]) + abs(v[1]) + abs(v[2])]
    for v in velocity_vectors
]


def extended(array, sides, width):
    for axis, dim in sides:
        count, length = (lax.axis_size(axis), array.shape[dim])
        up = [(i, (i + 1) % count) for i in range(count)]
        down = [(j, i) for i, j in up]
        last = lax.slice_in_dim(array, length - width, length, axis=dim)
        first = lax.slice_in_dim(array, 0, width, axis=dim)
        before = lax.ppermute(last, axis, up)
        after = lax.ppermute(first, axis, down)
        array = jnp.concatenate([before, array, after], axis=dim)
    return array


def column(table):
    return jnp.asarray(table, jnp.float32)[:, None, None]


def collide(pops, porosity, solid, drive):
    dir_x, dir_y, dir_z, wts = (column(vel_x), column(vel_y), column(vel_z), column(weight_table))
    fluid_density = jnp.sum(pops, 0)
    damp = 1.0 / (1.0 + porosity)
    vel_u = (jnp.sum(dir_x * pops, 0) / fluid_density + PUSH * drive) * damp
    vel_v = jnp.sum(dir_y * pops, 0) / fluid_density * damp
    vel_w = jnp.sum(dir_z * pops, 0) / fluid_density * damp
    along = dir_x * vel_u + dir_y * vel_v + dir_z * vel_w
    usq = vel_u * vel_u + vel_v * vel_v + vel_w * vel_w
    equil = wts * fluid_density * (1.0 + 3.0 * along + 4.5 * along * along - 1.5 * usq)
    fluid = pops - (pops - equil) / RELAX
    return jnp.where(solid[None] == 1, pops[::-1], fluid)


def energy(pops):
    fluid_density = jnp.sum(pops, 0)
    total_sum = jnp.zeros((), pops.dtype)
    for table in (vel_x, vel_y, vel_z):
        speed = jnp.sum(column(table) * pops, 0) / fluid_density
        total_sum = total_sum + 0.5 * jnp.sum(speed * speed)
    return total_sum


def roll_depth(piece, offset):
    if offset == 0:
        return piece
    depth_index = lax.broadcasted_iota(jnp.int32, piece.shape, piece.ndim - 1) % NZ
    if offset == 1:
        return jnp.where(
            depth_index == 0, jnp.roll(piece, -(NZ - 1), axis=-1), jnp.roll(piece, 1, axis=-1)
        )
    return jnp.where(
        depth_index == NZ - 1, jnp.roll(piece, NZ - 1, axis=-1), jnp.roll(piece, -1, axis=-1)
    )


def depth_layers(cube, sign):
    return jnp.stack([roll_depth(cube[:, :, level], sign * (level - 1)) for level in range(3)], 2)


def shrink_stream(padded, sign):
    rows_x = padded.shape[1] - 2
    width = padded.shape[2] - 2 * NZ
    cube = padded.reshape(3, 3, 3, padded.shape[1], padded.shape[2])
    first = jnp.stack(
        [cube[a, :, :, 1 - sign * (a - 1) : 1 - sign * (a - 1) + rows_x] for a in range(3)]
    )
    second = jnp.stack(
        [
            first[:, b, :, :, (1 - sign * (b - 1)) * NZ : (1 - sign * (b - 1)) * NZ + width]
            for b in range(3)
        ],
        1,
    )
    return depth_layers(second, sign).reshape(27, rows_x, width)


def stream(pops, sign):
    padx = extended(pops, (("gx", 1),), 1)
    pady = extended(padx, (("gy", 2),), NZ)
    return shrink_stream(pady, sign)


def on_device(populations, adjoint_in, porosity, solid, labels):
    drive = (labels == 1).astype(jnp.float32) - (labels == 2).astype(jnp.float32)
    states = []
    current = populations
    for step in range(STEPS):
        states.append(current)
        current = stream(collide(current, porosity, solid, drive), 1)
    adjoint_field = adjoint_in + jax.grad(energy)(current)
    total_sum = jnp.zeros_like(porosity)
    for step in range(STEPS - 1, -1, -1):
        pulled_values = stream(adjoint_field, -1)
        unused, backward_sweep = jax.vjp(
            lambda p, q: collide(p, q, solid, drive), states[step], porosity
        )
        adjoint_field, porosity_gradient = backward_sweep(pulled_values)
        total_sum = total_sum + porosity_gradient
    peak = lax.pmax(jnp.max(jnp.abs(total_sum)), ("gx", "gy"))
    return (current, adjoint_field, total_sum / (peak + EPS))


def solution(mesh):
    in_specs = (
        P(None, "gx", "gy"),
        P(None, "gx", "gy"),
        P("gx", "gy"),
        P("gx", "gy"),
        P("gx", "gy"),
    )
    out_specs = (P(None, "gx", "gy"), P(None, "gx", "gy"), P("gx", "gy"))
    return jax.shard_map(
        on_device, mesh=mesh, in_specs=in_specs, out_specs=out_specs, check_vma=False
    )
```

profile of v0, /device:TPU:0, one launch (start us, length us, event | category | flops | bytes accessed | tf_op | source)
XLA Modules:
  0.0 250.5 jit_solution(11300478272041487378)
XLA Ops:
  0.7 1.1 broadcast_compare_fusion.2
  1.8 3.1 %multiply_reduce_fusion.12 = (f32[32,1024]{1,0:T(8,128)S(1)}, f32[32,1024]{1,0:T(8,128)S(1)}, f32[32,1024]{1,0:T(8,128)S(1)}, f32[32,1024]{1,0:T(8,128)S(1)}) fusion(f32[27,32,1024]{2,1,0:T(8,128)} %param.24, f32[27]{0:T(128)} %constant.82.clone, f32[27]{0:T(128)} %constant.80.clone, f32[27]{0:T(128)} %constant.81.clone), kind=kLoop, calls=%fused_computation.106 | loop fusion | flops 6062080 | bytes 4063556 | tf_op jit(solution)/shard_map/reduce_sum | solution.py:46
  5.3 2.3 fusion.20
  8.0 5.1 %collective-permute-start.1 = (f32[27,1,1024]{2,0,1:T(8,128)S(1)}, f32[27,1,1024]{2,0,1:T(8,128)S(1)}, u32[]{:S(2)}, u32[]{:S(2)}) collective-permute-start(f32[27,1,1024]{2,0,1:T(8,128)S(1)} %copy.311), channel_id=1, source_target_pairs={{8,0},{16,8},{24,16},{0,24},{9,1},{17,9},{25,17},{1,25},{10,2},{18... | collective-permute-start | bytes 331784 | tf_op jit(solution)/shard_map/ppermute | solution.py:31
  13.2 3.8 %collective-permute-done.1 = f32[27,1,1024]{2,0,1:T(8,128)S(1)} collective-permute-done((f32[27,1,1024]{2,0,1:T(8,128)S(1)}, f32[27,1,1024]{2,0,1:T(8,128)S(1)}, u32[]{:S(2)}, u32[]{:S(2)}) %collective-permute-start.1) | collective-permute-done | bytes 110624 | tf_op jit(solution)/shard_map/ppermute | solution.py:31
  17.1 2.8 %collective-permute-done = f32[27,1,1024]{2,0,1:T(8,128)S(1)} collective-permute-done((f32[27,1,1024]{2,0,1:T(8,128)S(1)}, f32[27,1,1024]{2,0,1:T(8,128)S(1)}, u32[]{:S(2)}, u32[]{:S(2)}) %collective-permute-start) | collective-permute-done | bytes 110624 | tf_op jit(solution)/shard_map/ppermute | solution.py:30
  20.0 1.0 pad_maximum_fusion
  21.1 2.1 copy-done
  24.1 12.1 %collective-permute-done.3 = f32[27,34,64]{2,1,0:T(8,128)S(1)} collective-permute-done((f32[27,34,64]{2,1,0:T(8,128)S(1)}, f32[27,34,64]{2,1,0:T(8,128)S(1)}, u32[]{:S(2)}, u32[]{:S(2)}) %collective-permute-start.3) | collective-permute-done | bytes 235040 | tf_op jit(solution)/shard_map/ppermute | solution.py:31
  36.2 3.1 %collective-permute-done.2 = f32[27,34,64]{2,1,0:T(8,128)S(1)} collective-permute-done((f32[27,34,64]{2,1,0:T(8,128)S(1)}, f32[27,34,64]{2,1,0:T(8,128)S(1)}, u32[]{:S(2)}, u32[]{:S(2)}) %collective-permute-start.2) | collective-permute-done | bytes 235040 | tf_op jit(solution)/shard_map/ppermute | solution.py:30
  39.3 6.8 %concatenate.253 = f32[27,34,1152]{2,1,0:T(8,128)} concatenate(f32[27,34,64]{2,1,0:T(8,128)S(1)} %collective-permute-done.2, f32[27,34,1024]{2,1,0:T(8,128)} %copy-done, f32[27,34,64]{2,1,0:T(8,128)S(1)} %collective-permute-done.3), dimensions={2} | concatenate | bytes 8460288 | tf_op jit(solution)/shard_map/concatenate | solution.py:32
  46.1 2.8 %fusion.97 = (f32[1,3,3,32,1152]{4,3,2,1,0:T(8,128)S(1)}, f32[1,3,3,32,1152]{4,3,2,1,0:T(8,128)S(1)}, f32[1,3,3,32,1152]{4,3,2,1,0:T(8,128)S(1)}) fusion(f32[3,3,3,34,1152]{4,3,2,1,0:T(8,128)} %bitcast.144), kind=kLoop, calls=%fused_computation.225 | loop fusion | bytes 7962624 | tf_op jit(solution)/shard_map/slice | solution.py:85
  48.9 1.9 fusion.40
  52.4 0.9 fusion.89
  53.3 1.4 multiply_reduce_fusion.9
  54.9 2.3 fusion.27
  57.5 1.5 collective-permute-start.5
  59.6 4.2 %collective-permute-done.5 = f32[27,1,1024]{2,0,1:T(8,128)S(1)} collective-permute-done((f32[27,1,1024]{2,0,1:T(8,128)S(1)}, f32[27,1,1024]{2,0,1:T(8,128)S(1)}, u32[]{:S(2)}, u32[]{:S(2)}) %collective-permute-start.5) | collective-permute-done | bytes 110624 | tf_op jit(solution)/shard_map/ppermute | solution.py:31
  63.9 1.9 collective-permute-done.4
  66.0 1.0 pad_maximum_fusion.1
  67.0 2.1 copy-done.1
  69.4 0.7 collective-permute-start.6
  70.1 12.2 %collective-permute-done.7 = f32[27,34,64]{2,1,0:T(8,128)S(1)} collective-permute-done((f32[27,34,64]{2,1,0:T(8,128)S(1)}, f32[27,34,64]{2,1,0:T(8,128)S(1)}, u32[]{:S(2)}, u32[]{:S(2)}) %collective-permute-start.7) | collective-permute-done | bytes 235040 | tf_op jit(solution)/shard_map/ppermute | solution.py:31
  82.3 1.1 collective-permute-done.6
  83.4 6.8 %concatenate.267 = f32[27,34,1152]{2,1,0:T(8,128)} concatenate(f32[27,34,64]{2,1,0:T(8,128)S(1)} %collective-permute-done.6, f32[27,34,1024]{2,1,0:T(8,128)} %copy-done.1, f32[27,34,64]{2,1,0:T(8,128)S(1)} %collective-permute-done.7), dimensions={2} | concatenate | bytes 8460288 | tf_op jit(solution)/shard_map/concatenate | solution.py:32
  90.2 2.8 %fusion.96 = (f32[1,3,3,32,1152]{4,3,2,1,0:T(8,128)S(1)}, f32[1,3,3,32,1152]{4,3,2,1,0:T(8,128)S(1)}, f32[1,3,3,32,1152]{4,3,2,1,0:T(8,128)S(1)}) fusion(f32[3,3,3,34,1152]{4,3,2,1,0:T(8,128)} %bitcast.145), kind=kLoop, calls=%fused_computation.224 | loop fusion | bytes 7962624 | tf_op jit(solution)/shard_map/slice | solution.py:85
  93.0 1.9 fusion.32
  96.6 0.9 fusion.84
  97.5 2.7 %multiply_reduce_fusion.8 = (f32[32,1024]{1,0:T(8,128)S(1)}, f32[32,1024]{1,0:T(8,128)S(1)}, f32[32,1024]{1,0:T(8,128)S(1)}, f32[3,3,3,32,1024]{4,3,2,1,0:T(8,128)}) fusion(f32[3,3,3]{2,1,0:T(4,128)S(1)} %copy-done.51, f32[3,3,1,32,1024]{4,3,2,1,0:T(8,128)S(1)} %get-tuple-element.136, f32[3,3,1,32,1024]{4,3,2,1,0:T(8,128)S(1)} %get-tuple-element.106, ...), kind=kLoop, calls=%fused_computation.102 | loop fusion | flops 6979584 | bytes 7471428 | tf_op jit(solution)/shard_map/jvp()/reduce_sum | solution.py:58
  100.4 1.0 add_add_fusion.2
  101.6 2.3 collective-permute-start.9
  104.0 4.0 %collective-permute-done.9 = f32[27,1,1024]{2,0,1:T(8,128)S(1)} collective-permute-done((f32[27,1,1024]{2,0,1:T(8,128)S(1)}, f32[27,1,1024]{2,0,1:T(8,128)S(1)}, u32[]{:S(2)}, u32[]{:S(2)}) %collective-permute-start.9) | collective-permute-done | bytes 110624 | tf_op jit(solution)/shard_map/ppermute | solution.py:31
  108.1 2.6 %collective-permute-done.8 = f32[27,1,1024]{2,0,1:T(8,128)S(1)} collective-permute-done((f32[27,1,1024]{2,0,1:T(8,128)S(1)}, f32[27,1,1024]{2,0,1:T(8,128)S(1)}, u32[]{:S(2)}, u32[]{:S(2)}) %collective-permute-start.8) | collective-permute-done | bytes 110624 | tf_op jit(solution)/shard_map/ppermute | solution.py:30
  110.9 1.0 pad_maximum_fusion.2
  111.9 2.1 copy-done.2
  114.2 1.2 collective-permute-start.11
  115.8 12.0 %collective-permute-done.11 = f32[27,34,64]{2,1,0:T(8,128)S(1)} collective-permute-done((f32[27,34,64]{2,1,0:T(8,128)S(1)}, f32[27,34,64]{2,1,0:T(8,128)S(1)}, u32[]{:S(2)}, u32[]{:S(2)}) %collective-permute-start.11) | collective-permute-done | bytes 235040 | tf_op jit(solution)/shard_map/ppermute | solution.py:31
  127.8 1.7 collective-permute-done.10
  129.5 6.8 %concatenate.281 = f32[27,34,1152]{2,1,0:T(8,128)} concatenate(f32[27,34,64]{2,1,0:T(8,128)S(1)} %collective-permute-done.10, f32[27,34,1024]{2,1,0:T(8,128)} %copy-done.2, f32[27,34,64]{2,1,0:T(8,128)S(1)} %collective-permute-done.11), dimensions={2} | concatenate | bytes 8460288 | tf_op jit(solution)/shard_map/concatenate | solution.py:32
  136.3 2.8 %fusion.95 = (f32[1,3,3,32,1152]{4,3,2,1,0:T(8,128)S(1)}, f32[1,3,3,32,1152]{4,3,2,1,0:T(8,128)S(1)}, f32[1,3,3,32,1152]{4,3,2,1,0:T(8,128)S(1)}) fusion(f32[3,3,3,34,1152]{4,3,2,1,0:T(8,128)} %bitcast.146), kind=kLoop, calls=%fused_computation.223 | loop fusion | bytes 7962624 | tf_op jit(solution)/shard_map/slice | solution.py:85
  139.1 1.9 fusion.30
  142.6 0.8 fusion.49
  143.4 3.8 %multiply_reduce_fusion.5 = (f32[32,1024]{1,0:T(8,128)S(1)}, f32[32,1024]{1,0:T(8,128)S(1)}, f32[32,1024]{1,0:T(8,128)S(1)}, f32[32,1024]{1,0:T(8,128)S(1)}, f32...) fusion(f32[3,3,3]{2,1,0:T(4,128)S(1)} %copy-done.51, f32[3,3,3]{2,1,0:T(4,128)S(1)} %copy-done.53, ...), kind=kLoop, calls=%fused_computation.95 | loop fusion | flops 30801920 | bytes 8421808 | tf_op jit(solution)/shard_map/transpose(jvp())/reduce_sum | solution.py:47
  147.3 0.7 bitcast_select_fusion.3
  148.4 1.6 add_add_fusion.1
  150.2 1.9 collective-permute-start.13
  152.4 4.1 %collective-permute-done.13 = f32[27,1,1024]{2,0,1:T(8,128)S(1)} collective-permute-done((f32[27,1,1024]{2,0,1:T(8,128)S(1)}, f32[27,1,1024]{2,0,1:T(8,128)S(1)}, u32[]{:S(2)}, u32[]{:S(2)}) %collective-permute-start.13) | collective-permute-done | bytes 110624 | tf_op jit(solution)/shard_map/ppermute | solution.py:31
  156.6 2.3 collective-permute-done.12
  159.7 2.1 copy-done.3
  162.0 0.8 collective-permute-start.15
  163.0 12.4 %collective-permute-done.15 = f32[27,34,64]{2,1,0:T(8,128)S(1)} collective-permute-done((f32[27,34,64]{2,1,0:T(8,128)S(1)}, f32[27,34,64]{2,1,0:T(8,128)S(1)}, u32[]{:S(2)}, u32[]{:S(2)}) %collective-permute-start.15) | collective-permute-done | bytes 235040 | tf_op jit(solution)/shard_map/ppermute | solution.py:31
  175.5 1.7 collective-permute-done.14
  177.2 6.8 %concatenate.295 = f32[27,34,1152]{2,1,0:T(8,128)} concatenate(f32[27,34,64]{2,1,0:T(8,128)S(1)} %collective-permute-done.14, f32[27,34,1024]{2,1,0:T(8,128)} %copy-done.3, f32[27,34,64]{2,1,0:T(8,128)S(1)} %collective-permute-done.15), dimensions={2} | concatenate | bytes 8460288 | tf_op jit(solution)/shard_map/concatenate | solution.py:32
  184.0 2.8 %fusion.94 = (f32[1,3,3,32,1152]{4,3,2,1,0:T(8,128)S(1)}, f32[1,3,3,32,1152]{4,3,2,1,0:T(8,128)S(1)}, f32[1,3,3,32,1152]{4,3,2,1,0:T(8,128)S(1)}) fusion(f32[3,3,3,34,1152]{4,3,2,1,0:T(8,128)} %bitcast.147), kind=kLoop, calls=%fused_computation.222 | loop fusion | bytes 7962624 | tf_op jit(solution)/shard_map/slice | solution.py:85
  186.8 1.9 fusion.28
  190.4 0.8 fusion.48
  191.6 4.5 %multiply_reduce_fusion.2 = (f32[32,1024]{1,0:T(8,128)S(1)}, f32[32,1024]{1,0:T(8,128)S(1)}, f32[32,1024]{1,0:T(8,128)S(1)}, f32[32,1024]{1,0:T(8,128)S(1)}, f32...) fusion(f32[3,3,3]{2,1,0:T(4,128)S(1)} %copy-done.51, f32[3,3,3]{2,1,0:T(4,128)S(1)} %copy-done.54, ...), kind=kLoop, calls=%fused_computation.88 | loop fusion | flops 30801920 | bytes 8421808 | tf_op jit(solution)/shard_map/transpose(jvp())/reduce_sum | solution.py:47
  196.2 1.6 abs_reduce_fusion
  197.8 1.0 fusion.72
  198.8 39.1 %pmax.7 = f32[]{:T(128)} all-reduce(f32[]{:T(128)} %get-tuple-element.33), channel_id=1, replica_groups=mesh['gx'=4,'gy'=8] {'gx','gy'}, use_global_device_ids=true, to_apply=%region_33.34 | all-reduce | flops 1 | bytes 8 | tf_op jit(solution)/shard_map/pmax | solution.py:119
  237.9 3.2 %bitcast_select_fusion.1 = f32[27,32,1024]{2,1,0:T(8,128)} fusion(f32[3,3,3,32,1024]{4,3,2,1,0:T(8,128)S(1)} %get-tuple-element.92, pred[32,1024]{1,0:T(8,128)(4,1)} %copy-done.16), kind=kLoop, calls=%fused_computation.82 | loop fusion | flops 884736 | bytes 7110656 | tf_op jit(solution)/shard_map/transpose(jvp(jit(_where)))/select_n | solution.py:51
  241.6 1.6 broadcast_divide_fusion
  243.2 1.4 negate_add_fusion.1
  244.6 5.7 %add_add_fusion = f32[27,32,1024]{2,1,0:T(8,128)} fusion(f32[3,3,3,32,1024]{4,3,2,1,0:T(8,128)S(1)} %get-tuple-element.92, f32[27,32,1024]{2,1,0:T(8,128)} %bitcast_select_fusion.1, f32[32,1024]{1,0:T(8,128)S(1)} %negate_add_fusion.1, f32[32,1024]{1,0:T(8,128)} %get-tuple-element.120, f32[32,1024]{1,0:T(8,128)} %get-tuple-element.118, ...), kind=kLoop, calls=%fused_computation.85 | loop fusion | flops 10616832 | bytes 11174212 | tf_op jit(solution)/shard_map/transpose(jvp())/add_any | solution.py:42
  (201 shorter events, 13.5 us)
Async XLA Ops:
  0.6 4.6 %copy-start.57 = (f32[27]{0:T(128)S(1)}, f32[27]{0:T(128)}, u32[]{:S(2)}) copy-start(f32[27]{0:T(128)} %constant.82.clone) | copy-start | bytes 328
  0.6 4.6 %copy-start.59 = (f32[27]{0:T(128)S(1)}, f32[27]{0:T(128)}, u32[]{:S(2)}) copy-start(f32[27]{0:T(128)} %constant.81.clone) | copy-start | bytes 328
  0.7 4.6 %copy-start.61 = (f32[27]{0:T(128)S(1)}, f32[27]{0:T(128)}, u32[]{:S(2)}) copy-start(f32[27]{0:T(128)} %constant.80.clone) | copy-start | bytes 328
  0.7 4.6 %copy-start.63 = (f32[27]{0:T(128)S(1)}, f32[27]{0:T(128)}, u32[]{:S(2)}) copy-start(f32[27]{0:T(128)} %constant.83.clone) | copy-start | bytes 328
  0.7 4.6 %copy-start.4 = (f32[27,32,1024]{2,1,0:T(8,128)S(1)}, f32[27,32,1024]{2,1,0:T(8,128)}, u32[]{:S(2)}) copy-start(f32[27,32,1024]{2,1,0:T(8,128)} %param.24) | copy-start | bytes 10616836
  0.7 4.3 %copy-start.9 = (f32[32,1024]{1,0:T(8,128)S(1)}, f32[32,1024]{1,0:T(8,128)}, u32[]{:S(2)}) copy-start(f32[32,1024]{1,0:T(8,128)} %param.26) | copy-start | bytes 393220
  0.7 4.4 %copy-start.50 = (s32[32,1024]{1,0:T(8,128)S(1)}, s32[32,1024]{1,0:T(8,128)}, u32[]{:S(2)}) copy-start(s32[32,1024]{1,0:T(8,128)} %param.28) | copy-start | bytes 393220
  1.8 146.6 %copy-start.16 = (pred[32,1024]{1,0:T(8,128)(4,1)}, pred[32,1024]{1,0:T(8,128)(4,1)S(1)}, u32[]{:S(2)}) copy-start(pred[32,1024]{1,0:T(8,128)(4,1)S(1)} %broadcast_compare_fusion.2) | copy-start | bytes 98308
  4.9 2.7 %copy-start.5 = (f32[32,1024]{1,0:T(8,128)}, f32[32,1024]{1,0:T(8,128)S(1)}, u32[]{:S(2)}) copy-start(f32[32,1024]{1,0:T(8,128)S(1)} %get-tuple-element.27) | copy-start | bytes 393220
  4.9 2.7 %copy-start.20 = (f32[32,1024]{1,0:T(8,128)}, f32[32,1024]{1,0:T(8,128)S(1)}, u32[]{:S(2)}) copy-start(f32[32,1024]{1,0:T(8,128)S(1)} %get-tuple-element.26) | copy-start | bytes 393220
  5.0 2.7 %copy-start.44 = (f32[32,1024]{1,0:T(8,128)}, f32[32,1024]{1,0:T(8,128)S(1)}, u32[]{:S(2)}) copy-start(f32[32,1024]{1,0:T(8,128)S(1)} %get-tuple-element.25) | copy-start | bytes 393220
  5.0 2.7 %copy-start.45 = (f32[32,1024]{1,0:T(8,128)}, f32[32,1024]{1,0:T(8,128)S(1)}, u32[]{:S(2)}) copy-start(f32[32,1024]{1,0:T(8,128)S(1)} %get-tuple-element.28) | copy-start | bytes 393220
  5.1 2.7 %copy-start.24 = (f32[32,1024]{1,0:T(8,128)}, f32[32,1024]{1,0:T(8,128)S(1)}, u32[]{:S(2)}) copy-start(f32[32,1024]{1,0:T(8,128)S(1)} %get-tuple-element.67) | copy-start | bytes 393220
  5.1 2.7 %copy-start.26 = (f32[32,1024]{1,0:T(8,128)}, f32[32,1024]{1,0:T(8,128)S(1)}, u32[]{:S(2)}) copy-start(f32[32,1024]{1,0:T(8,128)S(1)} %get-tuple-element.130) | copy-start | bytes 393220
  5.1 2.7 %copy-start.32 = (f32[32,1024]{1,0:T(8,128)}, f32[32,1024]{1,0:T(8,128)S(1)}, u32[]{:S(2)}) copy-start(f32[32,1024]{1,0:T(8,128)S(1)} %get-tuple-element.66) | copy-start | bytes 393220
  5.1 2.7 %copy-start.34 = (f32[32,1024]{1,0:T(8,128)}, f32[32,1024]{1,0:T(8,128)S(1)}, u32[]{:S(2)}) copy-start(f32[32,1024]{1,0:T(8,128)S(1)} %get-tuple-element.129) | copy-start | bytes 393220
  5.2 2.5 %copy-start.12 = (f32[32,1024]{1,0:T(8,128)}, f32[32,1024]{1,0:T(8,128)S(1)}, u32[]{:S(2)}) copy-start(f32[32,1024]{1,0:T(8,128)S(1)} %get-tuple-element.69) | copy-start | bytes 393220
  5.2 2.5 %copy-start.30 = (f32[32,1024]{1,0:T(8,128)}, f32[32,1024]{1,0:T(8,128)S(1)}, u32[]{:S(2)}) copy-start(f32[32,1024]{1,0:T(8,128)S(1)} %get-tuple-element.68) | copy-start | bytes 393220
  5.3 49.6 %copy-start.46 = (pred[32,1024]{1,0:T(8,128)(4,1)}, pred[32,1024]{1,0:T(8,128)(4,1)S(1)}, u32[]{:S(2)}) copy-start(pred[32,1024]{1,0:T(8,128)(4,1)S(1)} %get-tuple-element.70) | copy-start | bytes 98308
  5.3 49.6 %copy-start.48 = (pred[32,1024]{1,0:T(8,128)(4,1)}, pred[32,1024]{1,0:T(8,128)(4,1)S(1)}, u32[]{:S(2)}) copy-start(pred[32,1024]{1,0:T(8,128)(4,1)S(1)} %get-tuple-element.71) | copy-start | bytes 98308
  8.0 9.0 %collective-permute-start.1 = (f32[27,1,1024]{2,0,1:T(8,128)S(1)}, f32[27,1,1024]{2,0,1:T(8,128)S(1)}, u32[]{:S(2)}, u32[]{:S(2)}) collective-permute-start(f32[27,1,1024]{2,0,1:T(8,128)S(1)} %copy.311), channel_id=1, source_target_pairs={{8,0},{16,8},{24,16},{0,24},{9,1},{17,9},{25,17},{1,25},{10,2},{18... | collective-permute-start | bytes 331784 | tf_op jit(solution)/shard_map/ppermute | solution.py:31
  13.1 6.8 %collective-permute-start = (f32[27,1,1024]{2,0,1:T(8,128)S(1)}, f32[27,1,1024]{2,0,1:T(8,128)S(1)}, u32[]{:S(2)}, u32[]{:S(2)}) collective-permute-start(f32[27,1,1024]{2,0,1:T(8,128)S(1)} %copy.310), channel_id=1, source_target_pairs={{0,8},{8,16},{16,24},{24,0},{1,9},{9,17},{17,25},{25,1},{2,10},{10... | collective-permute-start | bytes 331784 | tf_op jit(solution)/shard_map/ppermute | solution.py:30
  21.1 2.1 copy-start
  23.4 12.8 %collective-permute-start.3 = (f32[27,34,64]{2,1,0:T(8,128)S(1)}, f32[27,34,64]{2,1,0:T(8,128)S(1)}, u32[]{:S(2)}, u32[]{:S(2)}) collective-permute-start(f32[27,34,64]{2,1,0:T(8,128)S(1)} %get-tuple-element.90), channel_id=1, source_target_pairs={{1,0},{2,1},{3,2},{4,3},{5,4},{6,5},{7,6},{0,7},{9,8},{10,9},{11,1... | collective-permute-start | bytes 705032 | tf_op jit(solution)/shard_map/ppermute | solution.py:31
  23.9 15.4 %collective-permute-start.2 = (f32[27,34,64]{2,1,0:T(8,128)S(1)}, f32[27,34,64]{2,1,0:T(8,128)S(1)}, u32[]{:S(2)}, u32[]{:S(2)}) collective-permute-start(f32[27,34,64]{2,1,0:T(8,128)S(1)} %get-tuple-element.91), channel_id=1, source_target_pairs={{0,1},{1,2},{2,3},{3,4},{4,5},{5,6},{6,7},{7,0},{8,9},{9,10},{10,1... | collective-permute-start | bytes 705032 | tf_op jit(solution)/shard_map/ppermute | solution.py:30
  54.7 93.6 %copy-start.18 = (f32[32,1024]{1,0:T(8,128)}, f32[32,1024]{1,0:T(8,128)S(1)}, u32[]{:S(2)}) copy-start(f32[32,1024]{1,0:T(8,128)S(1)} %get-tuple-element.23) | copy-start | bytes 393220
  54.7 93.2 %copy-start.28 = (f32[32,1024]{1,0:T(8,128)}, f32[32,1024]{1,0:T(8,128)S(1)}, u32[]{:S(2)}) copy-start(f32[32,1024]{1,0:T(8,128)S(1)} %get-tuple-element.54) | copy-start | bytes 393220
  54.7 93.6 %copy-start.7 = (f32[32,1024]{1,0:T(8,128)}, f32[32,1024]{1,0:T(8,128)S(1)}, u32[]{:S(2)}) copy-start(f32[32,1024]{1,0:T(8,128)S(1)} %get-tuple-element.55) | copy-start | bytes 393220
  54.8 93.2 %copy-start.22 = (f32[32,1024]{1,0:T(8,128)}, f32[32,1024]{1,0:T(8,128)S(1)}, u32[]{:S(2)}) copy-start(f32[32,1024]{1,0:T(8,128)S(1)} %get-tuple-element.57) | copy-start | bytes 393220
  54.9 93.1 %copy-start.14 = (f32[32,1024]{1,0:T(8,128)}, f32[32,1024]{1,0:T(8,128)S(1)}, u32[]{:S(2)}) copy-start(f32[32,1024]{1,0:T(8,128)S(1)} %get-tuple-element.59) | copy-start | bytes 393220
  57.5 6.3 %collective-permute-start.5 = (f32[27,1,1024]{2,0,1:T(8,128)S(1)}, f32[27,1,1024]{2,0,1:T(8,128)S(1)}, u32[]{:S(2)}, u32[]{:S(2)}) collective-permute-start(f32[27,1,1024]{2,0,1:T(8,128)S(1)} %copy.335), channel_id=1, source_target_pairs={{8,0},{16,8},{24,16},{0,24},{9,1},{17,9},{25,17},{1,25},{10,2},{18... | collective-permute-start | bytes 331784 | tf_op jit(solution)/shard_map/ppermute | solution.py:31
  59.0 6.8 %collective-permute-start.4 = (f32[27,1,1024]{2,0,1:T(8,128)S(1)}, f32[27,1,1024]{2,0,1:T(8,128)S(1)}, u32[]{:S(2)}, u32[]{:S(2)}) collective-permute-start(f32[27,1,1024]{2,0,1:T(8,128)S(1)} %copy.334), channel_id=1, source_target_pairs={{0,8},{8,16},{16,24},{24,0},{1,9},{9,17},{17,25},{25,1},{2,10},{10... | collective-permute-start | bytes 331784 | tf_op jit(solution)/shard_map/ppermute | solution.py:30
  67.0 2.1 copy-start.1
  69.3 13.0 %collective-permute-start.7 = (f32[27,34,64]{2,1,0:T(8,128)S(1)}, f32[27,34,64]{2,1,0:T(8,128)S(1)}, u32[]{:S(2)}, u32[]{:S(2)}) collective-permute-start(f32[27,34,64]{2,1,0:T(8,128)S(1)} %get-tuple-element.88), channel_id=1, source_target_pairs={{1,0},{2,1},{3,2},{4,3},{5,4},{6,5},{7,6},{0,7},{9,8},{10,9},{11,1... | collective-permute-start | bytes 705032 | tf_op jit(solution)/shard_map/ppermute | solution.py:31
  69.4 14.0 %collective-permute-start.6 = (f32[27,34,64]{2,1,0:T(8,128)S(1)}, f32[27,34,64]{2,1,0:T(8,128)S(1)}, u32[]{:S(2)}, u32[]{:S(2)}) collective-permute-start(f32[27,34,64]{2,1,0:T(8,128)S(1)} %get-tuple-element.89), channel_id=1, source_target_pairs={{0,1},{1,2},{2,3},{3,4},{4,5},{5,6},{6,7},{7,0},{8,9},{9,10},{10,1... | collective-permute-start | bytes 705032 | tf_op jit(solution)/shard_map/ppermute | solution.py:30
  97.5 2.9 %copy-start.11 = (f32[27,32,1024]{2,1,0:T(8,128)S(1)}, f32[27,32,1024]{2,1,0:T(8,128)}, u32[]{:S(2)}) copy-start(f32[27,32,1024]{2,1,0:T(8,128)} %param.25) | copy-start | bytes 10616836
  101.6 6.4 %collective-permute-start.9 = (f32[27,1,1024]{2,0,1:T(8,128)S(1)}, f32[27,1,1024]{2,0,1:T(8,128)S(1)}, u32[]{:S(2)}, u32[]{:S(2)}) collective-permute-start(f32[27,1,1024]{2,0,1:T(8,128)S(1)} %copy.362), channel_id=1, source_target_pairs={{8,0},{16,8},{24,16},{0,24},{9,1},{17,9},{25,17},{1,25},{10,2},{18... | collective-permute-start | bytes 331784 | tf_op jit(solution)/shard_map/ppermute | solution.py:31
  104.0 6.8 %collective-permute-start.8 = (f32[27,1,1024]{2,0,1:T(8,128)S(1)}, f32[27,1,1024]{2,0,1:T(8,128)S(1)}, u32[]{:S(2)}, u32[]{:S(2)}) collective-permute-start(f32[27,1,1024]{2,0,1:T(8,128)S(1)} %copy.361), channel_id=1, source_target_pairs={{0,8},{8,16},{16,24},{24,0},{1,9},{9,17},{17,25},{25,1},{2,10},{10... | collective-permute-start | bytes 331784 | tf_op jit(solution)/shard_map/ppermute | solution.py:30
  111.9 2.1 copy-start.2
  114.2 13.5 %collective-permute-start.11 = (f32[27,34,64]{2,1,0:T(8,128)S(1)}, f32[27,34,64]{2,1,0:T(8,128)S(1)}, u32[]{:S(2)}, u32[]{:S(2)}) collective-permute-start(f32[27,34,64]{2,1,0:T(8,128)S(1)} %get-tuple-element.86), channel_id=1, source_target_pairs={{1,0},{2,1},{3,2},{4,3},{5,4},{6,5},{7,6},{0,7},{9,8},{10,9},{11,1... | collective-permute-start | bytes 705032 | tf_op jit(solution)/shard_map/ppermute | solution.py:31
  115.4 14.1 %collective-permute-start.10 = (f32[27,34,64]{2,1,0:T(8,128)S(1)}, f32[27,34,64]{2,1,0:T(8,128)S(1)}, u32[]{:S(2)}, u32[]{:S(2)}) collective-permute-start(f32[27,34,64]{2,1,0:T(8,128)S(1)} %get-tuple-element.87), channel_id=1, source_target_pairs={{0,1},{1,2},{2,3},{3,4},{4,5},{5,6},{6,7},{7,0},{8,9},{9,10},{10,1... | collective-permute-start | bytes 705032 | tf_op jit(solution)/shard_map/ppermute | solution.py:30
  150.2 6.3 %collective-permute-start.13 = (f32[27,1,1024]{2,0,1:T(8,128)S(1)}, f32[27,1,1024]{2,0,1:T(8,128)S(1)}, u32[]{:S(2)}, u32[]{:S(2)}) collective-permute-start(f32[27,1,1024]{2,0,1:T(8,128)S(1)} %copy.387), channel_id=1, source_target_pairs={{8,0},{16,8},{24,16},{0,24},{9,1},{17,9},{25,17},{1,25},{10,2},{18... | collective-permute-start | bytes 331784 | tf_op jit(solution)/shard_map/ppermute | solution.py:31
  152.1 6.8 %collective-permute-start.12 = (f32[27,1,1024]{2,0,1:T(8,128)S(1)}, f32[27,1,1024]{2,0,1:T(8,128)S(1)}, u32[]{:S(2)}, u32[]{:S(2)}) collective-permute-start(f32[27,1,1024]{2,0,1:T(8,128)S(1)} %copy.386), channel_id=1, source_target_pairs={{0,8},{8,16},{16,24},{24,0},{1,9},{9,17},{17,25},{25,1},{2,10},{10... | collective-permute-start | bytes 331784 | tf_op jit(solution)/shard_map/ppermute | solution.py:30
  159.7 2.1 copy-start.3
  162.0 13.4 %collective-permute-start.15 = (f32[27,34,64]{2,1,0:T(8,128)S(1)}, f32[27,34,64]{2,1,0:T(8,128)S(1)}, u32[]{:S(2)}, u32[]{:S(2)}) collective-permute-start(f32[27,34,64]{2,1,0:T(8,128)S(1)} %get-tuple-element.84), channel_id=1, source_target_pairs={{1,0},{2,1},{3,2},{4,3},{5,4},{6,5},{7,6},{0,7},{9,8},{10,9},{11,1... | collective-permute-start | bytes 705032 | tf_op jit(solution)/shard_map/ppermute | solution.py:31
  162.9 14.3 %collective-permute-start.14 = (f32[27,34,64]{2,1,0:T(8,128)S(1)}, f32[27,34,64]{2,1,0:T(8,128)S(1)}, u32[]{:S(2)}, u32[]{:S(2)}) collective-permute-start(f32[27,34,64]{2,1,0:T(8,128)S(1)} %get-tuple-element.85), channel_id=1, source_target_pairs={{0,1},{1,2},{2,3},{3,4},{4,5},{5,6},{6,7},{7,0},{8,9},{9,10},{10,1... | collective-permute-start | bytes 705032 | tf_op jit(solution)/shard_map/ppermute | solution.py:30
  191.5 4.6 %copy-start.8 = (f32[32,1024]{1,0:T(8,128)S(1)}, f32[32,1024]{1,0:T(8,128)}, u32[]{:S(2)}) copy-start(f32[32,1024]{1,0:T(8,128)} %copy-done.7) | copy-start | bytes 393220
  191.5 4.6 %copy-start.10 = (f32[32,1024]{1,0:T(8,128)S(1)}, f32[32,1024]{1,0:T(8,128)}, u32[]{:S(2)}) copy-start(f32[32,1024]{1,0:T(8,128)} %param.26) | copy-start | bytes 393220
  191.5 4.6 %copy-start.15 = (f32[32,1024]{1,0:T(8,128)S(1)}, f32[32,1024]{1,0:T(8,128)}, u32[]{:S(2)}) copy-start(f32[32,1024]{1,0:T(8,128)} %copy-done.14) | copy-start | bytes 393220
  191.5 4.6 %copy-start.19 = (f32[32,1024]{1,0:T(8,128)S(1)}, f32[32,1024]{1,0:T(8,128)}, u32[]{:S(2)}) copy-start(f32[32,1024]{1,0:T(8,128)} %copy-done.18) | copy-start | bytes 393220
  191.5 4.6 %copy-start.21 = (f32[32,1024]{1,0:T(8,128)S(1)}, f32[32,1024]{1,0:T(8,128)}, u32[]{:S(2)}) copy-start(f32[32,1024]{1,0:T(8,128)} %copy-done.20) | copy-start | bytes 393220
  191.5 4.6 %copy-start.23 = (f32[32,1024]{1,0:T(8,128)S(1)}, f32[32,1024]{1,0:T(8,128)}, u32[]{:S(2)}) copy-start(f32[32,1024]{1,0:T(8,128)} %copy-done.22) | copy-start | bytes 393220
  191.5 4.6 %copy-start.25 = (f32[32,1024]{1,0:T(8,128)S(1)}, f32[32,1024]{1,0:T(8,128)}, u32[]{:S(2)}) copy-start(f32[32,1024]{1,0:T(8,128)} %copy-done.24) | copy-start | bytes 393220
  191.6 4.6 %copy-start.27 = (f32[32,1024]{1,0:T(8,128)S(1)}, f32[32,1024]{1,0:T(8,128)}, u32[]{:S(2)}) copy-start(f32[32,1024]{1,0:T(8,128)} %copy-done.26) | copy-start | bytes 393220
  191.6 4.6 %copy-start.29 = (f32[32,1024]{1,0:T(8,128)S(1)}, f32[32,1024]{1,0:T(8,128)}, u32[]{:S(2)}) copy-start(f32[32,1024]{1,0:T(8,128)} %copy-done.28) | copy-start | bytes 393220
  191.6 4.6 %copy-start.37 = (f32[32,1024]{1,0:T(8,128)S(1)}, f32[32,1024]{1,0:T(8,128)}, u32[]{:S(2)}) copy-start(f32[32,1024]{1,0:T(8,128)} %copy-done.36) | copy-start | bytes 393220
  191.6 4.6 %copy-start.39 = (f32[32,1024]{1,0:T(8,128)S(1)}, f32[32,1024]{1,0:T(8,128)}, u32[]{:S(2)}) copy-start(f32[32,1024]{1,0:T(8,128)} %copy-done.38) | copy-start | bytes 393220
  191.6 4.6 %copy-start.41 = (f32[32,1024]{1,0:T(8,128)S(1)}, f32[32,1024]{1,0:T(8,128)}, u32[]{:S(2)}) copy-start(f32[32,1024]{1,0:T(8,128)} %copy-done.40) | copy-start | bytes 393220
  191.6 4.6 %copy-start.43 = (f32[32,1024]{1,0:T(8,128)S(1)}, f32[32,1024]{1,0:T(8,128)}, u32[]{:S(2)}) copy-start(f32[32,1024]{1,0:T(8,128)} %copy-done.42) | copy-start | bytes 393220
  191.6 4.6 %copy-start.47 = (pred[32,1024]{1,0:T(8,128)(4,1)S(1)}, pred[32,1024]{1,0:T(8,128)(4,1)}, u32[]{:S(2)}) copy-start(pred[32,1024]{1,0:T(8,128)(4,1)} %copy-done.46) | copy-start | bytes 98308
  191.6 4.6 %copy-start.49 = (pred[32,1024]{1,0:T(8,128)(4,1)S(1)}, pred[32,1024]{1,0:T(8,128)(4,1)}, u32[]{:S(2)}) copy-start(pred[32,1024]{1,0:T(8,128)(4,1)} %copy-done.48) | copy-start | bytes 98308
  237.9 6.7 %copy-start.58 = (f32[27]{0:T(128)S(1)}, f32[27]{0:T(128)}, u32[]{:S(2)}) copy-start(f32[27]{0:T(128)} %constant.82.clone) | copy-start | bytes 328
  237.9 6.7 %copy-start.60 = (f32[27]{0:T(128)S(1)}, f32[27]{0:T(128)}, u32[]{:S(2)}) copy-start(f32[27]{0:T(128)} %constant.81.clone) | copy-start | bytes 328
  237.9 6.7 %copy-start.62 = (f32[27]{0:T(128)S(1)}, f32[27]{0:T(128)}, u32[]{:S(2)}) copy-start(f32[27]{0:T(128)} %constant.80.clone) | copy-start | bytes 328
  (16 other events, 15.1 us)
where the time goes:
time: 255 us; the launch traced here: 250 us
  waiting for transfers between devices  82.2 us (32%)
  local copies, waits for them, and re-layouts  55.5 us (22%)
  other arithmetic  55.1 us (22%)
  blocking collectives  39.1 us (15%)
  starting transfers between devices  15.8 us (6%)
  between operations  2.82 us (1%)
    ppermute x8, waiting for transfers between devices, extended(): after = lax.ppermute(first, axis, down)  64.8 us
    pmax x1, blocking collectives, on_device(): peak = lax.pmax(jnp.max(jnp.abs(total_sum)), ('gx', 'gy'))  39.1 us
    concatenate x4, local copies, waits for them, and re-layouts, extended(): array = jnp.concatenate([before, array, after], axis=dim)  27.2 us
    ppermute x8, waiting for transfers between devices, extended(): before = lax.ppermute(last, axis, up)  17.4 us
    ppermute x8, starting transfers between devices, extended(): after = lax.ppermute(first, axis, down)  13.4 us
    slice x4, local copies, waits for them, and re-layouts, shrink_stream(): cube[a, :, :, 1 - sign * (a - 1):1 - sign * (a - 1) + rows_x]  11.2 us
    unnamed x128, local copies, waits for them, and re-layouts  9.15 us
    select_n x4, other arithmetic, collide(): return jnp.where(solid[None] == 1, pops[::-1], fluid)  8.52 us
  transfers between devices with their start and end apart: 16, of which 16 were waited for; matrix products, arithmetic and copies ran while one was open for 0% of the time, Pallas kernels for 0%

commit v1 on v0

v1 whole, which is shorter than its diff:
```python
import functools

import jax
import jax.numpy as jnp
from jax import lax
from jax.experimental import pallas as pl
from jax.experimental.pallas import tpu as pltpu
from jax.sharding import PartitionSpec as P

NZ = 64
RELAX = 0.8
PUSH = 0.2
EPS = 1e-06
LANES = 128
VELOCITY = [(a, b, c) for a in (-1, 0, 1) for b in (-1, 0, 1) for c in (-1, 0, 1)]
INDEX = {v: i for i, v in enumerate(VELOCITY)}
WEIGHT = [
    [8.0 / 27, 2.0 / 27, 1.0 / 54, 1.0 / 216][abs(v[0]) + abs(v[1]) + abs(v[2])]
    for v in VELOCITY
]
NORM = [abs(v[0]) + abs(v[1]) + abs(v[2]) for v in VELOCITY]
F32 = jnp.float32
VMEM_LIMIT = 20 * 1024 * 1024
CORNERS = [(1, 1), (1, -1), (-1, 1), (-1, -1)]


class Grid:
    def __init__(self, rows, width):
        self.rows = rows
        self.cols = width // LANES
        self.tiles = rows // 8
        self.panel = rows + 16
        self.padded = (27 * (self.cols + 1) * self.panel, LANES)

    def at(self, i, c, r):
        return (i * (self.cols + 1) + c) * self.panel + 8 + r


def scaled(d, sign):
    return (sign * d[0], sign * d[1], sign * d[2])


def lane_masks():
    lane = lax.broadcasted_iota(jnp.int32, (8, LANES), 1)
    return lane >= NZ, lane % NZ == 0, lane % NZ == NZ - 1


def pull(g, buf, i, d, c, r, masks):
    high, first, last = masks
    dx, dy, dz = d
    here = buf[pl.ds(g.at(i, c, r - dx), 8), :]
    if dy == 1:
        before = jnp.where(c == 0, g.cols, c - 1)
        here = jnp.where(high, buf[pl.ds(g.at(i, before, r - dx), 8), :], here)
    elif dy == -1:
        here = jnp.where(high, here, buf[pl.ds(g.at(i, c + 1, r - dx), 8), :])
    if dz == 0:
        return here if dy == 0 else pltpu.roll(here, NZ, 1)
    if dz == 1:
        one, other, edge = 1, NZ + 1, first
    else:
        one, other, edge = LANES - 1, NZ - 1, last
    inner, wrapped = (one, other) if dy == 0 else (other, one)
    return jnp.where(edge, pltpu.roll(here, wrapped, 1), pltpu.roll(here, inner, 1))


def moments(f):
    flat = {}
    along_z = None
    for a in (-1, 0, 1):
        for b in (-1, 0, 1):
            lo, mid, hi = (f[INDEX[(a, b, c)]] for c in (-1, 0, 1))
            flat[a, b] = lo + mid + hi
            diff = hi - lo
            along_z = diff if along_z is None else along_z + diff
    line = {}
    along_y = None
    for a in (-1, 0, 1):
        line[a] = flat[a, -1] + flat[a, 0] + flat[a, 1]
        diff = flat[a, 1] - flat[a, -1]
        along_y = diff if along_y is None else along_y + diff
    return line[-1] + line[0] + line[1], line[1] - line[-1], along_y, along_z


def combos(x, y, z):
    plane = {}
    for a in (-1, 0, 1):
        for b in (-1, 0, 1):
            if (a, b) > (0, 0):
                continue
            if a == 0:
                plane[a, b] = -y if b else None
            else:
                plane[a, b] = -x if b == 0 else (-x - y if b < 0 else y - x)
    out = []
    for a, b, c in VELOCITY[:13]:
        base = plane[a, b]
        if base is None:
            out.append(-z)
        else:
            out.append(base if c == 0 else (base - z if c < 0 else base + z))
    return out


def relax(f, rho, wx, wy, wz, damp, push, solid):
    ux, uy, uz = (wx + push) * damp, wy * damp, wz * damp
    base = 1.0 - 1.5 * (ux * ux + uy * uy + uz * uz)
    keep = 1.0 - 1.0 / RELAX
    gain = rho * (1.0 / RELAX)
    level = [gain * w for w in (8.0 / 27, 2.0 / 27, 1.0 / 54, 1.0 / 216)]
    along = combos(3.0 * ux, 3.0 * uy, 3.0 * uz)
    out = [None] * 27
    for i in range(13):
        j = 26 - i
        even = base + 0.5 * (along[i] * along[i])
        lift = level[NORM[i]]
        out[i] = jnp.where(solid, f[j], keep * f[i] + lift * (even + along[i]))
        out[j] = jnp.where(solid, f[i], keep * f[j] + lift * (even - along[i]))
    out[13] = jnp.where(solid, f[13], keep * f[13] + level[0] * base)
    return out


def pulled_moments(p):
    first = {}
    for a in (-1, 0, 1):
        for b in (-1, 0, 1):
            lo, mid, hi = (p[INDEX[(a, b, c)]] for c in (-1, 0, 1))
            both = lo + hi
            first[a, b] = (4.0 * mid + both, hi - lo, both)
    second = {}
    for a in (-1, 0, 1):
        lo, mid, hi = (first[a, b] for b in (-1, 0, 1))
        b0 = lo[0] + hi[0]
        b1 = lo[1] + hi[1]
        second[a] = dict(
            one=4.0 * mid[0] + b0,
            y=hi[0] - lo[0],
            yy=b0,
            z=4.0 * mid[1] + b1,
            yz=hi[1] - lo[1],
            zz=4.0 * mid[2] + lo[2] + hi[2],
        )
    lo, mid, hi = (second[a] for a in (-1, 0, 1))

    def full(key):
        return 4.0 * mid[key] + lo[key] + hi[key]

    xx = lo["one"] + hi["one"]
    return dict(
        one=4.0 * mid["one"] + xx,
        x=hi["one"] - lo["one"],
        xx=xx,
        y=full("y"),
        xy=hi["y"] - lo["y"],
        yy=full("yy"),
        z=full("z"),
        xz=hi["z"] - lo["z"],
        yz=full("yz"),
        zz=full("zz"),
    )


def adjoint_scalars(p, rho, wx, wy, wz, damp, push, solid):
    ux, uy, uz = (wx + push) * damp, wy * damp, wz * damp
    s = pulled_moments(p)
    scale = 1.0 / (216.0 * RELAX)
    one = s["one"] * scale
    b = [s[k] * (3.0 * scale) for k in ("x", "y", "z")]
    d = {k: s[k] * (9.0 * scale) for k in ("xx", "xy", "yy", "xz", "yz", "zz")}
    qx = d["xx"] * ux + d["xy"] * uy + d["xz"] * uz
    qy = d["xy"] * ux + d["yy"] * uy + d["yz"] * uz
    qz = d["xz"] * ux + d["yz"] * uy + d["zz"] * uz
    linear = b[0] * ux + b[1] * uy + b[2] * uz
    square = ux * ux + uy * uy + uz * uz
    even = one + linear + 0.5 * (qx * ux + qy * uy + qz * uz) - 1.5 * one * square
    three = 3.0 * one
    gx = (b[0] + qx - three * ux) * damp
    gy = (b[1] + qy - three * uy) * damp
    gz = (b[2] + qz - three * uz) * damp
    even = even - (gx * wx + gy * wy + gz * wz)
    porous = jnp.where(solid, 0.0, -rho * (gx * ux + gy * uy + gz * uz))
    return even, gx, gy, gz, porous


def adjoint_spread(p, even, gx, gy, gz, solid):
    keep = 1.0 - 1.0 / RELAX
    along = combos(gx, gy, gz)
    out = [None] * 27
    for i in range(13):
        j = 26 - i
        out[i] = jnp.where(solid, p[j], keep * p[i] + (even + along[i]))
        out[j] = jnp.where(solid, p[i], keep * p[j] + (even - along[i]))
    out[13] = jnp.where(solid, p[13], keep * p[13] + even)
    return out


def faces(sign, axis, side):
    return [i for i, v in enumerate(VELOCITY) if sign * v[axis] == side]


def corner(sign, sx, sy):
    return [i for i, v in enumerate(VELOCITY) if sign * v[0] == sx and sign * v[1] == sy]


def fill_sends(g, buf, sign, sends, high):
    x_up, x_down, y_up, y_down = sends[:4]
    for side, ref in ((1, x_up), (-1, x_down)):
        row = g.rows - 1 if side == 1 else 0
        for k, i in enumerate(faces(sign, 0, side)):
            ref[k * g.cols : (k + 1) * g.cols, :] = buf[
                pl.ds(g.at(i, 0, row), g.cols, stride=g.panel), :
            ]
    for side, ref in ((1, y_up), (-1, y_down)):
        col = g.cols - 1 if side == 1 else 0
        pops = faces(sign, 1, side)
        for k in range(5):
            for a in range(g.tiles):
                value = buf[pl.ds(g.at(pops[k], col, 8 * a), 8), :]
                if k < 4:
                    other = pltpu.roll(buf[pl.ds(g.at(pops[5 + k], col, 8 * a), 8), :], NZ, 1)
                    pair = (value, other) if side == 1 else (other, value)
                    value = jnp.where(high, *pair)
                ref[k * g.rows + 8 * a : k * g.rows + 8 * a + 8, :] = value
    for (sx, sy), ref in zip(CORNERS, sends[4:]):
        row = g.rows - 1 if sx == 1 else 0
        col = g.cols - 1 if sy == 1 else 0
        ref[...] = jnp.zeros((8, LANES), F32)
        for k, i in enumerate(corner(sign, sx, sy)):
            ref[k : k + 1, :] = buf[pl.ds(g.at(i, col, row), 1), :]


def fill_halo(g, buf, sign, parcels):
    x_up, x_down, y_up, y_down = parcels[:4]
    for side, ref in ((1, x_up), (-1, x_down)):
        row = -1 if side == 1 else g.rows
        for k, i in enumerate(faces(sign, 0, side)):
            buf[pl.ds(g.at(i, 0, row), g.cols, stride=g.panel), :] = ref[
                k * g.cols : (k + 1) * g.cols, :
            ]
    for side, ref in ((1, y_up), (-1, y_down)):
        pops = faces(sign, 1, side)
        for k in range(5):
            for a in range(g.tiles):
                value = ref[k * g.rows + 8 * a : k * g.rows + 8 * a + 8, :]
                buf[pl.ds(g.at(pops[k], g.cols, 8 * a), 8), :] = value
                if k < 4:
                    buf[pl.ds(g.at(pops[5 + k], g.cols, 8 * a), 8), :] = pltpu.roll(value, NZ, 1)
    for (sx, sy), ref in zip(CORNERS, parcels[4:]):
        row = -1 if sx == 1 else g.rows
        for k, i in enumerate(corner(sign, sx, sy)):
            buf[pl.ds(g.at(i, g.cols, row), 1), :] = ref[k : k + 1, :]


def tile_of(g, ref, k, c, r):
    return ref[pl.ds((k * g.cols + c) * g.rows + r, 8), :]


def put_tile(g, ref, k, c, r, value):
    ref[pl.ds((k * g.cols + c) * g.rows + r, 8), :] = value


def over_tiles(g, body, before=None, after=None):
    def column(c, carry):
        if before is not None:
            before(c)

        def tile(a, inner):
            body(c, pl.multiple_of(a * 8, 8))
            return inner

        lax.fori_loop(0, g.tiles, tile, 0)
        if after is not None:
            after(c)
        return carry

    lax.fori_loop(0, g.cols, column, 0)


def save_state(g, ref, c, r, rho, wx, wy, wz):
    for k, value in enumerate((rho, wx, wy, wz)):
        put_tile(g, ref, k, c, r, value)


def read_aux(g, aux, c, r):
    return tile_of(g, aux, 0, c, r), tile_of(g, aux, 1, c, r), tile_of(g, aux, 2, c, r) > 0.5


def first_kernel(g, pops, porosity, solid, labels, out, state, aux, *rest):
    sends, (stage, sems) = rest[:8], rest[8:]
    high = lane_masks()[0]

    def copy(c):
        source = pops.at[:, :, pl.ds(pl.multiple_of(c * LANES, LANES), LANES)]
        return pltpu.make_async_copy(source, stage.at[c], sems.at[c])

    for c in range(g.cols):
        copy(c).start()

    def body(c, r):
        f = [stage[c, i, pl.ds(r, 8), :] for i in range(27)]
        spot = (pl.ds(r, 8), pl.ds(pl.multiple_of(c * LANES, LANES), LANES))
        wall = solid[spot]
        label = labels[spot]
        damp = 1.0 / (1.0 + porosity[spot])
        push = jnp.where(label == 1, PUSH, jnp.where(label == 2, -PUSH, 0.0))
        put_tile(g, aux, 0, c, r, damp)
        put_tile(g, aux, 1, c, r, push)
        put_tile(g, aux, 2, c, r, wall.astype(F32))
        rho, mx, my, mz = moments(f)
        inverse = 1.0 / rho
        wx, wy, wz = mx * inverse, my * inverse, mz * inverse
        save_state(g, state, c, r, rho, wx, wy, wz)
        for i, value in enumerate(relax(f, rho, wx, wy, wz, damp, push, wall == 1)):
            out[pl.ds(g.at(i, c, r), 8), :] = value

    over_tiles(g, body, before=lambda c: copy(c).wait())
    fill_sends(g, out, 1, sends, high)


def second_kernel(g, padded, aux, *rest):
    parcels, (buf, out, state), sends = rest[:8], rest[8:11], rest[11:19]
    del padded
    masks = lane_masks()
    fill_halo(g, buf, 1, parcels)

    def body(c, r):
        f = [pull(g, buf, i, VELOCITY[i], c, r, masks) for i in range(27)]
        damp, push, wall = read_aux(g, aux, c, r)
        rho, mx, my, mz = moments(f)
        inverse = 1.0 / rho
        wx, wy, wz = mx * inverse, my * inverse, mz * inverse
        save_state(g, state, c, r, rho, wx, wy, wz)
        for i, value in enumerate(relax(f, rho, wx, wy, wz, damp, push, wall)):
            out[pl.ds(g.at(i, c, r), 8), :] = value

    over_tiles(g, body)
    fill_sends(g, out, 1, sends, masks[0])


def third_kernel(g, padded, adjoint, *rest):
    parcels, (final, buf, out), sends = rest[:8], rest[8:11], rest[11:19]
    stage_out, stage_in, sems_out, sems_in = rest[19:]
    del padded
    masks = lane_masks()

    def block(ref, c):
        return ref.at[:, :, pl.ds(pl.multiple_of(c * LANES, LANES), LANES)]

    def copy_in(c):
        return pltpu.make_async_copy(block(adjoint, c), stage_in.at[c], sems_in.at[c])

    def copy_out(c):
        return pltpu.make_async_copy(stage_out.at[c], block(final, c), sems_out.at[c])

    for c in range(g.cols):
        copy_in(c).start()
    fill_halo(g, buf, 1, parcels)

    def body(c, r):
        f = [pull(g, buf, i, VELOCITY[i], c, r, masks) for i in range(27)]
        for i in range(27):
            stage_out[c, i, pl.ds(r, 8), :] = f[i]
        rho, mx, my, mz = moments(f)
        inverse = 1.0 / rho
        wx, wy, wz = mx * inverse, my * inverse, mz * inverse
        even = -(wx * wx + wy * wy + wz * wz) * inverse
        along = combos(wx * inverse, wy * inverse, wz * inverse)
        for i in range(27):
            value = stage_in[c, i, pl.ds(r, 8), :] + even
            if i < 13:
                value = value + along[i]
            elif i > 13:
                value = value - along[26 - i]
            out[pl.ds(g.at(i, c, r), 8), :] = value

    over_tiles(
        g, body, before=lambda c: copy_in(c).wait(), after=lambda c: copy_out(c).start()
    )
    fill_sends(g, out, -1, sends, masks[0])
    for c in range(g.cols):
        copy_out(c).wait()


def fourth_kernel(g, padded, state, aux, *rest):
    parcels, (buf, out, total), sends = rest[:8], rest[8:11], rest[11:19]
    del padded
    masks = lane_masks()
    fill_halo(g, buf, -1, parcels)

    def body(c, r):
        p = [pull(g, buf, i, scaled(VELOCITY[i], -1), c, r, masks) for i in range(27)]
        damp, push, wall = read_aux(g, aux, c, r)
        rho, wx, wy, wz = (tile_of(g, state, k, c, r) for k in range(4))
        even, gx, gy, gz, porous = adjoint_scalars(p, rho, wx, wy, wz, damp, push, wall)
        put_tile(g, total, 0, c, r, porous)
        for i, value in enumerate(adjoint_spread(p, even, gx, gy, gz, wall)):
            out[pl.ds(g.at(i, c, r), 8), :] = value

    over_tiles(g, body)
    fill_sends(g, out, -1, sends, masks[0])


def fifth_kernel(g, padded, state, aux, before, *rest):
    parcels, (result, buf, total, peak) = rest[:8], rest[8:12]
    stage_out, sems_out = rest[12:]
    del padded
    masks = lane_masks()

    def copy_out(c):
        target = result.at[:, :, pl.ds(pl.multiple_of(c * LANES, LANES), LANES)]
        return pltpu.make_async_copy(stage_out.at[c], target, sems_out.at[c])

    fill_halo(g, buf, -1, parcels)
    peak[...] = jnp.zeros((8, LANES), F32)

    def body(c, r):
        p = [pull(g, buf, i, scaled(VELOCITY[i], -1), c, r, masks) for i in range(27)]
        damp, push, wall = read_aux(g, aux, c, r)
        rho, wx, wy, wz = (tile_of(g, state, k, c, r) for k in range(4))
        even, gx, gy, gz, porous = adjoint_scalars(p, rho, wx, wy, wz, damp, push, wall)
        here = tile_of(g, before, 0, c, r) + porous
        put_tile(g, total, 0, c, r, here)
        peak[...] = jnp.maximum(peak[...], jnp.abs(here))
        for i, value in enumerate(adjoint_spread(p, even, gx, gy, gz, wall)):
            stage_out[c, i, pl.ds(r, 8), :] = value

    over_tiles(g, body, after=lambda c: copy_out(c).start())
    for c in range(g.cols):
        copy_out(c).wait()


def scale_kernel(g, total, peak, out):
    largest = jnp.max(peak[...])
    factor = 1.0 / (jnp.full((8, LANES), largest, F32) + EPS)

    for c in range(g.cols):
        for a in range(g.tiles):
            out[8 * a : 8 * a + 8, c * LANES : (c + 1) * LANES] = (
                tile_of(g, total, 0, c, 8 * a) * factor
            )


def ring(mesh_axes, sizes, shift):
    nx, ny = sizes
    sx, sy = shift
    if mesh_axes == "gx":
        return [(i, (i + sx) % nx) for i in range(nx)]
    if mesh_axes == "gy":
        return [(i, (i + sy) % ny) for i in range(ny)]
    return [
        (x * ny + y, ((x + sx) % nx) * ny + (y + sy) % ny)
        for x in range(nx)
        for y in range(ny)
    ]


def exchange(sends, sizes):
    moves = [("gx", (1, 0)), ("gx", (-1, 0)), ("gy", (0, 1)), ("gy", (0, -1))]
    moves += [(("gx", "gy"), shift) for shift in CORNERS]
    return [
        lax.ppermute(parcel, axes, ring(axes, sizes, shift))
        for parcel, (axes, shift) in zip(sends, moves)
    ]


def largest_of_all(peak, sizes):
    nx, ny = sizes
    for axis, count in (("gy", ny), ("gx", nx)):
        parts = [peak]
        for k in range(1, count):
            parts.append(lax.ppermute(peak, axis, ring(axis, sizes, (k, k))))
        peak = functools.reduce(jnp.maximum, parts)
    return peak


def on_device(sizes, populations, adjoint_in, porosity, solid, labels):
    rows, width = porosity.shape
    g = Grid(rows, width)
    in_vmem = pl.BlockSpec(memory_space=pltpu.VMEM)
    anywhere = pl.BlockSpec(memory_space=pl.ANY)
    hbm = pl.BlockSpec(memory_space=pltpu.HBM)
    padded = pltpu.VMEM(g.padded, F32)

    def fields(count):
        return pltpu.VMEM((count * g.cols * rows, LANES), F32)

    parcel_shapes = [
        pltpu.VMEM((9 * g.cols, LANES), F32),
        pltpu.VMEM((9 * g.cols, LANES), F32),
        pltpu.VMEM((5 * rows, LANES), F32),
        pltpu.VMEM((5 * rows, LANES), F32),
    ] + [pltpu.VMEM((8, LANES), F32)] * 4
    whole = jax.ShapeDtypeStruct(populations.shape, F32)
    stage = pltpu.VMEM((g.cols, 27, rows, LANES), F32)
    sems = pltpu.SemaphoreType.DMA((g.cols,))

    def call(kernel, in_specs, out_shape, out_specs, scratch=(), aliases=None, name=None):
        return pl.pallas_call(
            functools.partial(kernel, g),
            in_specs=in_specs,
            out_shape=out_shape,
            out_specs=out_specs,
            scratch_shapes=list(scratch),
            input_output_aliases=aliases or {},
            compiler_params=pltpu.CompilerParams(vmem_limit_bytes=VMEM_LIMIT),
            name=name,
        )

    def pin(x):
        return pltpu.with_memory_space_constraint(x, pltpu.VMEM)

    post, state0, aux, *sends = call(
        first_kernel,
        [anywhere, in_vmem, in_vmem, in_vmem],
        [padded, fields(4), fields(3)] + parcel_shapes,
        [in_vmem] * 11,
        [stage, sems],
        name="collide_first",
    )(populations, porosity, solid, labels)
    parcels = exchange(sends, sizes)

    _, post, state1, *sends = call(
        second_kernel,
        [in_vmem] * 10,
        [padded, padded, fields(4)] + parcel_shapes,
        [in_vmem] * 11,
        aliases={0: 0},
        name="collide_second",
    )(pin(post), pin(aux), *parcels)
    parcels = exchange(sends, sizes)

    final, _, field, *sends = call(
        third_kernel,
        [in_vmem, anywhere] + [in_vmem] * 8,
        [whole, padded, padded] + parcel_shapes,
        [hbm] + [in_vmem] * 10,
        [stage, stage, sems, sems],
        aliases={0: 1},
        name="stream_and_seed",
    )(pin(post), adjoint_in, *parcels)
    parcels = exchange(sends, sizes)

    _, field, total, *sends = call(
        fourth_kernel,
        [in_vmem] * 11,
        [padded, padded, fields(1)] + parcel_shapes,
        [in_vmem] * 11,
        aliases={0: 0},
        name="adjoint_second",
    )(pin(field), pin(state1), pin(aux), *parcels)
    parcels = exchange(sends, sizes)

    adjoint_out, _, total, peak = call(
        fifth_kernel,
        [in_vmem] * 12,
        [whole, padded, fields(1), pltpu.VMEM((8, LANES), F32)],
        [hbm] + [in_vmem] * 3,
        [stage, sems],
        aliases={0: 1},
        name="adjoint_first",
    )(pin(field), pin(state0), pin(aux), pin(total), *parcels)

    peak = largest_of_all(peak, sizes)
    sensitivity = call(
        scale_kernel,
        [in_vmem, in_vmem],
        jax.ShapeDtypeStruct(porosity.shape, F32),
        in_vmem,
        name="normalize",
    )(pin(total), peak)
    return final, adjoint_out, sensitivity


def solution(mesh):
    sizes = (mesh.shape["gx"], mesh.shape["gy"])
    whole, flat = P(None, "gx", "gy"), P("gx", "gy")
    return jax.shard_map(
        functools.partial(on_device, sizes),
        mesh=mesh,
        in_specs=(whole, whole, flat, flat, flat),
        out_specs=(whole, whole, flat),
        check_vma=False,
    )
```

time: 255 us -> 155 us (0.61); the launches traced: 250 us -> 155 us
  other arithmetic: 55.1 us -> 0.01 us
  local copies, waits for them, and re-layouts: 55.5 us -> 4.71 us
  blocking collectives: 39.1 us -> 0 us
  Pallas kernels: 0 us -> 25.2 us
  starting transfers between devices: 15.8 us -> 38.6 us
  waiting for transfers between devices: 82.2 us -> 85.7 us
    pmax x1 -> x0, blocking collectives: 39.1 us -> none  [on_device(): peak = lax.pmax(jnp.max(jnp.abs(total_sum)), ('gx', 'gy'))]
    concatenate x32 -> x0, local copies, waits for them, and re-layouts: 31.8 us -> none  [the longest x4 27.2 us: extended(): array = jnp.concatenate([before, array, after], axis=dim)]
    pallas_call x0 -> x6, Pallas kernels: none -> 25.2 us  [the longest x1 5.97 us: on_device(): call(third_kernel, [in_vmem, anywhere] + [in_vmem] * 8, [whole, padded, p...]
    ppermute x16 -> x42, starting transfers between devices: 15.8 us -> 38.6 us  [the longest x32 27.6 us: exchange(): lax.ppermute(parcel, axes, ring(axes, sizes, shift))]
    reduce_sum x9 -> x0, other arithmetic: 18.2 us -> none  [the longest x2 8.28 us: collide(): along = dir_x * vel_u + dir_y * vel_v + dir_z * vel_w]
    slice x20 -> x0, local copies, waits for them, and re-layouts: 12.9 us -> none  [the longest x4 11.2 us: shrink_stream(): cube[a, :, :, 1 - sign * (a - 1):1 - sign * (a - 1) + rows_x]]
    select_n x6 -> x0, other arithmetic: 10 us -> none  [the longest x4 8.52 us: collide(): return jnp.where(solid[None] == 1, pops[::-1], fluid)]
    add_any x4 -> x0, other arithmetic: 8.74 us -> none  [the longest x2 7.29 us: collide(): fluid_density = jnp.sum(pops, 0)]
  transfers between devices with their start and end apart: 16 -> 42, of which waited for: 16 -> 21; matrix products, arithmetic and copies ran while one was open for 0% -> 0% of each run, Pallas kernels for 0% -> 0%
where the time goes in v1:
time: 155 us
  waiting for transfers between devices  85.7 us (55%)
  starting transfers between devices  38.6 us (25%)
  Pallas kernels  25.2 us (16%)
  local copies, waits for them, and re-layouts  4.71 us (3%)
    ppermute x32, waiting for transfers between devices, exchange(): lax.ppermute(parcel, axes, ring(axes, sizes, shift))  77 us
    ppermute x32, starting transfers between devices, exchange(): lax.ppermute(parcel, axes, ring(axes, sizes, shift))  27.6 us
    ppermute x10, starting transfers between devices, largest_of_all(): parts.append(lax.ppermute(peak, axis, ring(axis, sizes, (k, k))))  11 us
    ppermute x10, waiting for transfers between devices, largest_of_all(): parts.append(lax.ppermute(peak, axis, ring(axis, sizes, (k, k))))  8.68 us
    pallas_call x1, Pallas kernels, on_device(): call(third_kernel, [in_vmem, anywhere] + [in_vmem] * 8, [whole, padded, p...  5.97 us
    pallas_call x1, Pallas kernels, on_device(): call(fifth_kernel, [in_vmem] * 12, [whole, padded, fields(1), pltpu.VMEM(...  5.84 us
    pallas_call x1, Pallas kernels, on_device(): call(second_kernel, [in_vmem] * 10, [padded, padded, fields(4)] + parcel_...  5.15 us
    pallas_call x1, Pallas kernels, on_device(): call(fourth_kernel, [in_vmem] * 11, [padded, padded, fields(1)] + parcel_...  4.98 us
  transfers between devices with their start and end apart: 42, of which 21 were waited for; matrix products, arithmetic and copies ran while one was open for 0% of the time, Pallas kernels for 0%

profile of v1, /device:TPU:0, one launch (start us, length us, event | category | flops | bytes accessed | tf_op | source)
XLA Modules:
  0.0 155.1 jit_solution(18180015109533233041)
XLA Ops:
  0.6 2.0 %copy-done.1 = f32[27,32,1024]{2,1,0:T(8,128)S(1)} copy-done((f32[27,32,1024]{2,1,0:T(8,128)S(1)}, f32[27,32,1024]{2,1,0:T(8,128)}, u32[]{:S(2)}) %copy-start.1) | copy-done | bytes 3538968
  2.6 0.9 copy-done.2
  3.5 0.9 copy-done.3
  4.4 0.9 copy-done.4
  5.3 2.5 %collide_first.1 = (f32[11664,128]{1,0:T(8,128)S(1)}, f32[1024,128]{1,0:T(8,128)S(1)}, f32[768,128]{1,0:T(8,128)S(1)}, f32[72,128]{1,0:T(8,128)S(1)}, f32[72,128...) custom-call(f32[27,32,1024]{2,1,0:T(8,128)S(1)} %copy-done.1, ...), custom_call_target="tpu_custom_call" | custom-call | tf_op jit(solution)/shard_map/collide_first/pallas_call | solution.py:512
  7.9 0.5 collective-permute-start.2
  8.4 2.9 %collective-permute-start.3 = (f32[160,128]{1,0:T(8,128)S(1)}, f32[160,128]{1,0:T(8,128)S(1)}, u32[]{:S(2)}, u32[]{:S(2)}) collective-permute-start(f32[160,128]{1,0:T(8,128)S(1)} %get-tuple-element.52), channel_id=1, source_target_pairs={{0,7},{1,0},{2,1},{3,2},{4,3},{5,4},{6,5},{7,6},{8,15},{9,8},{10,9... | collective-permute-start | bytes 245768 | tf_op jit(solution)/shard_map/ppermute | solution.py:461
  11.3 2.3 %collective-permute-start = (f32[72,128]{1,0:T(8,128)S(1)}, f32[72,128]{1,0:T(8,128)S(1)}, u32[]{:S(2)}, u32[]{:S(2)}) collective-permute-start(f32[72,128]{1,0:T(8,128)S(1)} %get-tuple-element.49), channel_id=1, source_target_pairs={{0,8},{8,16},{16,24},{24,0},{1,9},{9,17},{17,25},{25,1},{2,10},{10... | collective-permute-start | bytes 110600 | tf_op jit(solution)/shard_map/ppermute | solution.py:461
  13.6 2.0 %collective-permute-start.1 = (f32[72,128]{1,0:T(8,128)S(1)}, f32[72,128]{1,0:T(8,128)S(1)}, u32[]{:S(2)}, u32[]{:S(2)}) collective-permute-start(f32[72,128]{1,0:T(8,128)S(1)} %get-tuple-element.50), channel_id=1, source_target_pairs={{0,24},{8,0},{16,8},{24,16},{1,25},{9,1},{17,9},{25,17},{2,26},{10... | collective-permute-start | bytes 110600 | tf_op jit(solution)/shard_map/ppermute | solution.py:461
  15.6 0.0 collective-permute-start.4
  15.6 6.6 %collective-permute-done.4.rest_4_ = f32[8,128]{1,0:T(8,128)S(1)} collective-permute-done((f32[8,128]{1,0:T(8,128)S(1)}, f32[8,128]{1,0:T(8,128)S(1)}, u32[]{:S(2)}, u32[]{:S(2)}) %collective-permute-start.4) | collective-permute-done | bytes 4128 | tf_op jit(solution)/shard_map/ppermute | solution.py:461
  22.3 4.8 %collective-permute-done.5.rest_5_ = f32[8,128]{1,0:T(8,128)S(1)} collective-permute-done((f32[8,128]{1,0:T(8,128)S(1)}, f32[8,128]{1,0:T(8,128)S(1)}, u32[]{:S(2)}, u32[]{:S(2)}) %collective-permute-start.5) | collective-permute-done | bytes 4128 | tf_op jit(solution)/shard_map/ppermute | solution.py:461
  27.1 0.0 collective-permute-start.6
  27.1 4.8 %collective-permute-done.6.rest_6_ = f32[8,128]{1,0:T(8,128)S(1)} collective-permute-done((f32[8,128]{1,0:T(8,128)S(1)}, f32[8,128]{1,0:T(8,128)S(1)}, u32[]{:S(2)}, u32[]{:S(2)}) %collective-permute-start.6) | collective-permute-done | bytes 4128 | tf_op jit(solution)/shard_map/ppermute | solution.py:461
  31.9 0.3 collective-permute-start.7
  32.2 2.7 %collective-permute-done.7.rest_7_ = f32[8,128]{1,0:T(8,128)S(1)} collective-permute-done((f32[8,128]{1,0:T(8,128)S(1)}, f32[8,128]{1,0:T(8,128)S(1)}, u32[]{:S(2)}, u32[]{:S(2)}) %collective-permute-start.7) | collective-permute-done | bytes 4128 | tf_op jit(solution)/shard_map/ppermute | solution.py:461
  35.0 0.0 collective-permute-done.1.rest_1_
  35.0 0.0 collective-permute-done.2.rest_2_
  35.0 0.0 collective-permute-done.3.rest_3_
  35.0 5.2 %collide_second.1 = (f32[11664,128]{1,0:T(8,128)S(1)}, f32[11664,128]{1,0:T(8,128)S(1)}, f32[1024,128]{1,0:T(8,128)S(1)}, f32[72,128]{1,0:T(8,128)S(1)}, f32[72,...) custom-call(f32[11664,128]{1,0:T(8,128)S(1)} %get-tuple-element.47.p, ...), custom_call_target="tpu_custom_call", output_to_operand_aliasing={{0}: (0, {})} | custom-call | tf_op jit(solution)/shard_map/collide_second/pallas_call | solution.py:522
  40.1 0.1 collective-permute-start.10
  40.2 2.6 %collective-permute-start.11 = (f32[160,128]{1,0:T(8,128)S(1)}, f32[160,128]{1,0:T(8,128)S(1)}, u32[]{:S(2)}, u32[]{:S(2)}) collective-permute-start(f32[160,128]{1,0:T(8,128)S(1)} %get-tuple-element.61), channel_id=1, source_target_pairs={{0,7},{1,0},{2,1},{3,2},{4,3},{5,4},{6,5},{7,6},{8,15},{9,8},{10,9... | collective-permute-start | bytes 245768 | tf_op jit(solution)/shard_map/ppermute | solution.py:461
  42.8 0.0 collective-permute-start.8
  42.8 3.8 %collective-permute-start.9 = (f32[72,128]{1,0:T(8,128)S(1)}, f32[72,128]{1,0:T(8,128)S(1)}, u32[]{:S(2)}, u32[]{:S(2)}) collective-permute-start(f32[72,128]{1,0:T(8,128)S(1)} %get-tuple-element.59), channel_id=1, source_target_pairs={{0,24},{8,0},{16,8},{24,16},{1,25},{9,1},{17,9},{25,17},{2,26},{10... | collective-permute-start | bytes 110600 | tf_op jit(solution)/shard_map/ppermute | solution.py:461
  46.7 0.0 collective-permute-start.12
  46.7 6.6 %collective-permute-done.12.rest_4_ = f32[8,128]{1,0:T(8,128)S(1)} collective-permute-done((f32[8,128]{1,0:T(8,128)S(1)}, f32[8,128]{1,0:T(8,128)S(1)}, u32[]{:S(2)}, u32[]{:S(2)}) %collective-permute-start.12) | collective-permute-done | bytes 4128 | tf_op jit(solution)/shard_map/ppermute | solution.py:461
  53.3 4.8 %collective-permute-done.13.rest_5_ = f32[8,128]{1,0:T(8,128)S(1)} collective-permute-done((f32[8,128]{1,0:T(8,128)S(1)}, f32[8,128]{1,0:T(8,128)S(1)}, u32[]{:S(2)}, u32[]{:S(2)}) %collective-permute-start.13) | collective-permute-done | bytes 4128 | tf_op jit(solution)/shard_map/ppermute | solution.py:461
  58.1 0.0 collective-permute-start.14
  58.1 4.8 %collective-permute-done.14.rest_6_ = f32[8,128]{1,0:T(8,128)S(1)} collective-permute-done((f32[8,128]{1,0:T(8,128)S(1)}, f32[8,128]{1,0:T(8,128)S(1)}, u32[]{:S(2)}, u32[]{:S(2)}) %collective-permute-start.14) | collective-permute-done | bytes 4128 | tf_op jit(solution)/shard_map/ppermute | solution.py:461
  63.0 3.0 %collective-permute-done.15.rest_7_ = f32[8,128]{1,0:T(8,128)S(1)} collective-permute-done((f32[8,128]{1,0:T(8,128)S(1)}, f32[8,128]{1,0:T(8,128)S(1)}, u32[]{:S(2)}, u32[]{:S(2)}) %collective-permute-start.15) | collective-permute-done | bytes 4128 | tf_op jit(solution)/shard_map/ppermute | solution.py:461
  66.0 0.0 collective-permute-done.11.rest_3_
  66.0 6.0 %stream_and_seed.1 = (f32[27,32,1024]{2,1,0:T(8,128)}, f32[11664,128]{1,0:T(8,128)S(1)}, f32[11664,128]{1,0:T(8,128)S(1)}, f32[72,128]{1,0:T(8,128)S(1)}, f32[72...) custom-call(f32[11664,128]{1,0:T(8,128)S(1)} %get-tuple-element.57.p, ...), custom_call_target="tpu_custom_call", output_to_operand_aliasing={{1}: (0, {})} | custom-call | tf_op jit(solution)/shard_map/stream_and_seed/pallas_call | solution.py:532
  72.0 0.1 collective-permute-start.18
  72.1 2.6 %collective-permute-start.19 = (f32[160,128]{1,0:T(8,128)S(1)}, f32[160,128]{1,0:T(8,128)S(1)}, u32[]{:S(2)}, u32[]{:S(2)}) collective-permute-start(f32[160,128]{1,0:T(8,128)S(1)} %get-tuple-element.72), channel_id=1, source_target_pairs={{0,7},{1,0},{2,1},{3,2},{4,3},{5,4},{6,5},{7,6},{8,15},{9,8},{10,9... | collective-permute-start | bytes 245768 | tf_op jit(solution)/shard_map/ppermute | solution.py:461
  74.7 3.8 %collective-permute-start.17 = (f32[72,128]{1,0:T(8,128)S(1)}, f32[72,128]{1,0:T(8,128)S(1)}, u32[]{:S(2)}, u32[]{:S(2)}) collective-permute-start(f32[72,128]{1,0:T(8,128)S(1)} %get-tuple-element.70), channel_id=1, source_target_pairs={{0,24},{8,0},{16,8},{24,16},{1,25},{9,1},{17,9},{25,17},{2,26},{10... | collective-permute-start | bytes 110600 | tf_op jit(solution)/shard_map/ppermute | solution.py:461
  78.5 6.6 %collective-permute-done.20.rest_4_ = f32[8,128]{1,0:T(8,128)S(1)} collective-permute-done((f32[8,128]{1,0:T(8,128)S(1)}, f32[8,128]{1,0:T(8,128)S(1)}, u32[]{:S(2)}, u32[]{:S(2)}) %collective-permute-start.20) | collective-permute-done | bytes 4128 | tf_op jit(solution)/shard_map/ppermute | solution.py:461
  85.1 0.0 collective-permute-start.21
  85.1 4.8 %collective-permute-done.21.rest_5_ = f32[8,128]{1,0:T(8,128)S(1)} collective-permute-done((f32[8,128]{1,0:T(8,128)S(1)}, f32[8,128]{1,0:T(8,128)S(1)}, u32[]{:S(2)}, u32[]{:S(2)}) %collective-permute-start.21) | collective-permute-done | bytes 4128 | tf_op jit(solution)/shard_map/ppermute | solution.py:461
  90.0 4.8 %collective-permute-done.22.rest_6_ = f32[8,128]{1,0:T(8,128)S(1)} collective-permute-done((f32[8,128]{1,0:T(8,128)S(1)}, f32[8,128]{1,0:T(8,128)S(1)}, u32[]{:S(2)}, u32[]{:S(2)}) %collective-permute-start.22) | collective-permute-done | bytes 4128 | tf_op jit(solution)/shard_map/ppermute | solution.py:461
  94.8 0.0 collective-permute-start.23
  94.8 3.0 %collective-permute-done.23.rest_7_ = f32[8,128]{1,0:T(8,128)S(1)} collective-permute-done((f32[8,128]{1,0:T(8,128)S(1)}, f32[8,128]{1,0:T(8,128)S(1)}, u32[]{:S(2)}, u32[]{:S(2)}) %collective-permute-start.23) | collective-permute-done | bytes 4128 | tf_op jit(solution)/shard_map/ppermute | solution.py:461
  97.9 5.0 %adjoint_second.1 = (f32[11664,128]{1,0:T(8,128)S(1)}, f32[11664,128]{1,0:T(8,128)S(1)}, f32[256,128]{1,0:T(8,128)S(1)}, f32[72,128]{1,0:T(8,128)S(1)}, f32[72,1...) custom-call(f32[11664,128]{1,0:T(8,128)S(1)} %get-tuple-element.67.p, ...), custom_call_target="tpu_custom_call", output_to_operand_aliasing={{0}: (0, {})} | custom-call | tf_op jit(solution)/shard_map/adjoint_second/pallas_call | solution.py:543
  102.8 0.1 collective-permute-start.26
  102.9 2.6 %collective-permute-start.27 = (f32[160,128]{1,0:T(8,128)S(1)}, f32[160,128]{1,0:T(8,128)S(1)}, u32[]{:S(2)}, u32[]{:S(2)}) collective-permute-start(f32[160,128]{1,0:T(8,128)S(1)} %get-tuple-element.83), channel_id=1, source_target_pairs={{0,7},{1,0},{2,1},{3,2},{4,3},{5,4},{6,5},{7,6},{8,15},{9,8},{10,9... | collective-permute-start | bytes 245768 | tf_op jit(solution)/shard_map/ppermute | solution.py:461
  105.5 3.8 %collective-permute-start.25 = (f32[72,128]{1,0:T(8,128)S(1)}, f32[72,128]{1,0:T(8,128)S(1)}, u32[]{:S(2)}, u32[]{:S(2)}) collective-permute-start(f32[72,128]{1,0:T(8,128)S(1)} %get-tuple-element.81), channel_id=1, source_target_pairs={{0,24},{8,0},{16,8},{24,16},{1,25},{9,1},{17,9},{25,17},{2,26},{10... | collective-permute-start | bytes 110600 | tf_op jit(solution)/shard_map/ppermute | solution.py:461
  109.4 6.6 %collective-permute-done.28.rest_4_ = f32[8,128]{1,0:T(8,128)S(1)} collective-permute-done((f32[8,128]{1,0:T(8,128)S(1)}, f32[8,128]{1,0:T(8,128)S(1)}, u32[]{:S(2)}, u32[]{:S(2)}) %collective-permute-start.28) | collective-permute-done | bytes 4128 | tf_op jit(solution)/shard_map/ppermute | solution.py:461
  116.0 4.8 %collective-permute-done.29.rest_5_ = f32[8,128]{1,0:T(8,128)S(1)} collective-permute-done((f32[8,128]{1,0:T(8,128)S(1)}, f32[8,128]{1,0:T(8,128)S(1)}, u32[]{:S(2)}, u32[]{:S(2)}) %collective-permute-start.29) | collective-permute-done | bytes 4128 | tf_op jit(solution)/shard_map/ppermute | solution.py:461
  120.8 4.8 %collective-permute-done.30.rest_6_ = f32[8,128]{1,0:T(8,128)S(1)} collective-permute-done((f32[8,128]{1,0:T(8,128)S(1)}, f32[8,128]{1,0:T(8,128)S(1)}, u32[]{:S(2)}, u32[]{:S(2)}) %collective-permute-start.30) | collective-permute-done | bytes 4128 | tf_op jit(solution)/shard_map/ppermute | solution.py:461
  125.7 3.0 %collective-permute-done.31.rest_7_ = f32[8,128]{1,0:T(8,128)S(1)} collective-permute-done((f32[8,128]{1,0:T(8,128)S(1)}, f32[8,128]{1,0:T(8,128)S(1)}, u32[]{:S(2)}, u32[]{:S(2)}) %collective-permute-start.31) | collective-permute-done | bytes 4128 | tf_op jit(solution)/shard_map/ppermute | solution.py:461
  128.7 5.8 %adjoint_first.1 = (f32[27,32,1024]{2,1,0:T(8,128)}, f32[11664,128]{1,0:T(8,128)S(1)}, f32[256,128]{1,0:T(8,128)S(1)}, f32[8,128]{1,0:T(8,128)S(1)}) custom-call(f32[11664,128]{1,0:T(8,128)S(1)} %get-tuple-element.77.padded, f32[1024,128]{1,0:T(8,128)S(1)} %get-tuple-element.78.state, ...), custom_call_target="tpu_custom_call", output_to_operand_aliasing={{1}: (0, {})} | custom-call | tf_op jit(solution)/shard_map/adjoint_first/pallas_call | solution.py:553
  134.6 0.1 collective-permute-start.38
  134.6 1.0 collective-permute-start.37
  135.6 0.9 collective-permute-start.36
  136.4 0.9 collective-permute-start.35
  137.4 0.6 collective-permute-start.34
  138.0 2.8 %collective-permute-start.33 = (f32[8,128]{1,0:T(8,128)S(1)}, f32[8,128]{1,0:T(8,128)S(1)}, u32[]{:S(2)}, u32[]{:S(2)}) collective-permute-start(f32[8,128]{1,0:T(8,128)S(1)} %get-tuple-element.90), channel_id=1, source_target_pairs={{0,2},{1,3},{2,4},{3,5},{4,6},{5,7},{6,0},{7,1},{8,10},{9,11},{10,... | collective-permute-start | bytes 12296 | tf_op jit(solution)/shard_map/ppermute | solution.py:471
  140.8 1.6 %collective-permute-done.33 = f32[8,128]{1,0:T(8,128)S(1)} collective-permute-done((f32[8,128]{1,0:T(8,128)S(1)}, f32[8,128]{1,0:T(8,128)S(1)}, u32[]{:S(2)}, u32[]{:S(2)}) %collective-permute-start.33) | collective-permute-done | bytes 4128 | tf_op jit(solution)/shard_map/ppermute | solution.py:471
  142.5 2.3 %collective-permute-done.32 = f32[8,128]{1,0:T(8,128)S(1)} collective-permute-done((f32[8,128]{1,0:T(8,128)S(1)}, f32[8,128]{1,0:T(8,128)S(1)}, u32[]{:S(2)}, u32[]{:S(2)}) %collective-permute-start.32) | collective-permute-done | bytes 4128 | tf_op jit(solution)/shard_map/ppermute | solution.py:471
  144.7 4.2 %collective-permute-start.41 = (f32[8,128]{1,0:T(8,128)S(1)}, f32[8,128]{1,0:T(8,128)S(1)}, u32[]{:S(2)}, u32[]{:S(2)}) collective-permute-start(f32[8,128]{1,0:T(8,128)S(1)} %maximum_maximum_fusion.1), channel_id=1, source_target_pairs={{0,24},{8,0},{16,8},{24,16},{1,25},{9,1},{17,9},{25,17},{2,26},{10... | collective-permute-start | bytes 12296 | tf_op jit(solution)/shard_map/ppermute | solution.py:471
  148.9 0.6 collective-permute-start.39
  149.5 0.7 collective-permute-done.41
  150.2 3.2 %collective-permute-done.40 = f32[8,128]{1,0:T(8,128)S(1)} collective-permute-done((f32[8,128]{1,0:T(8,128)S(1)}, f32[8,128]{1,0:T(8,128)S(1)}, u32[]{:S(2)}, u32[]{:S(2)}) %collective-permute-start.40) | collective-permute-done | bytes 4128 | tf_op jit(solution)/shard_map/ppermute | solution.py:471
  153.4 0.9 collective-permute-done.39
  154.3 0.8 normalize.1
  (38 shorter events, 0.1 us)
Async XLA Ops:
  0.6 2.0 %copy-start.1 = (f32[27,32,1024]{2,1,0:T(8,128)S(1)}, f32[27,32,1024]{2,1,0:T(8,128)}, u32[]{:S(2)}) copy-start(f32[27,32,1024]{2,1,0:T(8,128)} %pops.1) | copy-start | bytes 10616836
  2.6 0.9 copy-start.2
  3.5 0.9 copy-start.3
  4.4 0.9 copy-start.4
  5.3 60.7 %copy-start = (f32[27,32,1024]{2,1,0:T(8,128)S(1)}, f32[27,32,1024]{2,1,0:T(8,128)}, u32[]{:S(2)}) copy-start(f32[27,32,1024]{2,1,0:T(8,128)} %adjoint.1) | copy-start | bytes 10616836
  7.9 27.1 %collective-permute-start.2 = (f32[160,128]{1,0:T(8,128)S(1)}, f32[160,128]{1,0:T(8,128)S(1)}, u32[]{:S(2)}, u32[]{:S(2)}) collective-permute-start(f32[160,128]{1,0:T(8,128)S(1)} %get-tuple-element.51), channel_id=1, source_target_pairs={{0,1},{1,2},{2,3},{3,4},{4,5},{5,6},{6,7},{7,0},{8,9},{9,10},{10,1... | collective-permute-start | bytes 245768 | tf_op jit(solution)/shard_map/ppermute | solution.py:461
  8.4 26.6 %collective-permute-start.3 = (f32[160,128]{1,0:T(8,128)S(1)}, f32[160,128]{1,0:T(8,128)S(1)}, u32[]{:S(2)}, u32[]{:S(2)}) collective-permute-start(f32[160,128]{1,0:T(8,128)S(1)} %get-tuple-element.52), channel_id=1, source_target_pairs={{0,7},{1,0},{2,1},{3,2},{4,3},{5,4},{6,5},{7,6},{8,15},{9,8},{10,9... | collective-permute-start | bytes 245768 | tf_op jit(solution)/shard_map/ppermute | solution.py:461
  11.3 23.6 %collective-permute-start = (f32[72,128]{1,0:T(8,128)S(1)}, f32[72,128]{1,0:T(8,128)S(1)}, u32[]{:S(2)}, u32[]{:S(2)}) collective-permute-start(f32[72,128]{1,0:T(8,128)S(1)} %get-tuple-element.49), channel_id=1, source_target_pairs={{0,8},{8,16},{16,24},{24,0},{1,9},{9,17},{17,25},{25,1},{2,10},{10... | collective-permute-start | bytes 110600 | tf_op jit(solution)/shard_map/ppermute | solution.py:461
  13.6 21.4 %collective-permute-start.1 = (f32[72,128]{1,0:T(8,128)S(1)}, f32[72,128]{1,0:T(8,128)S(1)}, u32[]{:S(2)}, u32[]{:S(2)}) collective-permute-start(f32[72,128]{1,0:T(8,128)S(1)} %get-tuple-element.50), channel_id=1, source_target_pairs={{0,24},{8,0},{16,8},{24,16},{1,25},{9,1},{17,9},{25,17},{2,26},{10... | collective-permute-start | bytes 110600 | tf_op jit(solution)/shard_map/ppermute | solution.py:461
  15.6 6.6 %collective-permute-start.4 = (f32[8,128]{1,0:T(8,128)S(1)}, f32[8,128]{1,0:T(8,128)S(1)}, u32[]{:S(2)}, u32[]{:S(2)}) collective-permute-start(f32[8,128]{1,0:T(8,128)S(1)} %get-tuple-element.53), channel_id=1, source_target_pairs={{0,9},{1,10},{2,11},{3,12},{4,13},{5,14},{6,15},{7,8},{8,17},{9,18... | collective-permute-start | bytes 12296 | tf_op jit(solution)/shard_map/ppermute | solution.py:461
  22.2 4.8 %collective-permute-start.5 = (f32[8,128]{1,0:T(8,128)S(1)}, f32[8,128]{1,0:T(8,128)S(1)}, u32[]{:S(2)}, u32[]{:S(2)}) collective-permute-start(f32[8,128]{1,0:T(8,128)S(1)} %get-tuple-element.54), channel_id=1, source_target_pairs={{0,15},{1,8},{2,9},{3,10},{4,11},{5,12},{6,13},{7,14},{8,23},{9,16... | collective-permute-start | bytes 12296 | tf_op jit(solution)/shard_map/ppermute | solution.py:461
  27.1 4.8 %collective-permute-start.6 = (f32[8,128]{1,0:T(8,128)S(1)}, f32[8,128]{1,0:T(8,128)S(1)}, u32[]{:S(2)}, u32[]{:S(2)}) collective-permute-start(f32[8,128]{1,0:T(8,128)S(1)} %get-tuple-element.55), channel_id=1, source_target_pairs={{0,25},{1,26},{2,27},{3,28},{4,29},{5,30},{6,31},{7,24},{8,1},{9,2... | collective-permute-start | bytes 12296 | tf_op jit(solution)/shard_map/ppermute | solution.py:461
  31.9 3.0 %collective-permute-start.7 = (f32[8,128]{1,0:T(8,128)S(1)}, f32[8,128]{1,0:T(8,128)S(1)}, u32[]{:S(2)}, u32[]{:S(2)}) collective-permute-start(f32[8,128]{1,0:T(8,128)S(1)} %get-tuple-element.56), channel_id=1, source_target_pairs={{0,31},{1,24},{2,25},{3,26},{4,27},{5,28},{6,29},{7,30},{8,7},{9,0... | collective-permute-start | bytes 12296 | tf_op jit(solution)/shard_map/ppermute | solution.py:461
  40.1 25.9 %collective-permute-start.10 = (f32[160,128]{1,0:T(8,128)S(1)}, f32[160,128]{1,0:T(8,128)S(1)}, u32[]{:S(2)}, u32[]{:S(2)}) collective-permute-start(f32[160,128]{1,0:T(8,128)S(1)} %get-tuple-element.60), channel_id=1, source_target_pairs={{0,1},{1,2},{2,3},{3,4},{4,5},{5,6},{6,7},{7,0},{8,9},{9,10},{10,1... | collective-permute-start | bytes 245768 | tf_op jit(solution)/shard_map/ppermute | solution.py:461
  40.2 25.8 %collective-permute-start.11 = (f32[160,128]{1,0:T(8,128)S(1)}, f32[160,128]{1,0:T(8,128)S(1)}, u32[]{:S(2)}, u32[]{:S(2)}) collective-permute-start(f32[160,128]{1,0:T(8,128)S(1)} %get-tuple-element.61), channel_id=1, source_target_pairs={{0,7},{1,0},{2,1},{3,2},{4,3},{5,4},{6,5},{7,6},{8,15},{9,8},{10,9... | collective-permute-start | bytes 245768 | tf_op jit(solution)/shard_map/ppermute | solution.py:461
  42.8 23.2 %collective-permute-start.8 = (f32[72,128]{1,0:T(8,128)S(1)}, f32[72,128]{1,0:T(8,128)S(1)}, u32[]{:S(2)}, u32[]{:S(2)}) collective-permute-start(f32[72,128]{1,0:T(8,128)S(1)} %get-tuple-element.58), channel_id=1, source_target_pairs={{0,8},{8,16},{16,24},{24,0},{1,9},{9,17},{17,25},{25,1},{2,10},{10... | collective-permute-start | bytes 110600 | tf_op jit(solution)/shard_map/ppermute | solution.py:461
  42.8 23.2 %collective-permute-start.9 = (f32[72,128]{1,0:T(8,128)S(1)}, f32[72,128]{1,0:T(8,128)S(1)}, u32[]{:S(2)}, u32[]{:S(2)}) collective-permute-start(f32[72,128]{1,0:T(8,128)S(1)} %get-tuple-element.59), channel_id=1, source_target_pairs={{0,24},{8,0},{16,8},{24,16},{1,25},{9,1},{17,9},{25,17},{2,26},{10... | collective-permute-start | bytes 110600 | tf_op jit(solution)/shard_map/ppermute | solution.py:461
  46.7 6.6 %collective-permute-start.12 = (f32[8,128]{1,0:T(8,128)S(1)}, f32[8,128]{1,0:T(8,128)S(1)}, u32[]{:S(2)}, u32[]{:S(2)}) collective-permute-start(f32[8,128]{1,0:T(8,128)S(1)} %get-tuple-element.62), channel_id=1, source_target_pairs={{0,9},{1,10},{2,11},{3,12},{4,13},{5,14},{6,15},{7,8},{8,17},{9,18... | collective-permute-start | bytes 12296 | tf_op jit(solution)/shard_map/ppermute | solution.py:461
  53.3 4.8 %collective-permute-start.13 = (f32[8,128]{1,0:T(8,128)S(1)}, f32[8,128]{1,0:T(8,128)S(1)}, u32[]{:S(2)}, u32[]{:S(2)}) collective-permute-start(f32[8,128]{1,0:T(8,128)S(1)} %get-tuple-element.63), channel_id=1, source_target_pairs={{0,15},{1,8},{2,9},{3,10},{4,11},{5,12},{6,13},{7,14},{8,23},{9,16... | collective-permute-start | bytes 12296 | tf_op jit(solution)/shard_map/ppermute | solution.py:461
  58.1 4.8 %collective-permute-start.14 = (f32[8,128]{1,0:T(8,128)S(1)}, f32[8,128]{1,0:T(8,128)S(1)}, u32[]{:S(2)}, u32[]{:S(2)}) collective-permute-start(f32[8,128]{1,0:T(8,128)S(1)} %get-tuple-element.64), channel_id=1, source_target_pairs={{0,25},{1,26},{2,27},{3,28},{4,29},{5,30},{6,31},{7,24},{8,1},{9,2... | collective-permute-start | bytes 12296 | tf_op jit(solution)/shard_map/ppermute | solution.py:461
  63.0 3.0 %collective-permute-start.15 = (f32[8,128]{1,0:T(8,128)S(1)}, f32[8,128]{1,0:T(8,128)S(1)}, u32[]{:S(2)}, u32[]{:S(2)}) collective-permute-start(f32[8,128]{1,0:T(8,128)S(1)} %get-tuple-element.65), channel_id=1, source_target_pairs={{0,31},{1,24},{2,25},{3,26},{4,27},{5,28},{6,29},{7,30},{8,7},{9,0... | collective-permute-start | bytes 12296 | tf_op jit(solution)/shard_map/ppermute | solution.py:461
  72.0 25.9 %collective-permute-start.18 = (f32[160,128]{1,0:T(8,128)S(1)}, f32[160,128]{1,0:T(8,128)S(1)}, u32[]{:S(2)}, u32[]{:S(2)}) collective-permute-start(f32[160,128]{1,0:T(8,128)S(1)} %get-tuple-element.71), channel_id=1, source_target_pairs={{0,1},{1,2},{2,3},{3,4},{4,5},{5,6},{6,7},{7,0},{8,9},{9,10},{10,1... | collective-permute-start | bytes 245768 | tf_op jit(solution)/shard_map/ppermute | solution.py:461
  72.1 25.8 %collective-permute-start.19 = (f32[160,128]{1,0:T(8,128)S(1)}, f32[160,128]{1,0:T(8,128)S(1)}, u32[]{:S(2)}, u32[]{:S(2)}) collective-permute-start(f32[160,128]{1,0:T(8,128)S(1)} %get-tuple-element.72), channel_id=1, source_target_pairs={{0,7},{1,0},{2,1},{3,2},{4,3},{5,4},{6,5},{7,6},{8,15},{9,8},{10,9... | collective-permute-start | bytes 245768 | tf_op jit(solution)/shard_map/ppermute | solution.py:461
  74.7 23.2 %collective-permute-start.16 = (f32[72,128]{1,0:T(8,128)S(1)}, f32[72,128]{1,0:T(8,128)S(1)}, u32[]{:S(2)}, u32[]{:S(2)}) collective-permute-start(f32[72,128]{1,0:T(8,128)S(1)} %get-tuple-element.69), channel_id=1, source_target_pairs={{0,8},{8,16},{16,24},{24,0},{1,9},{9,17},{17,25},{25,1},{2,10},{10... | collective-permute-start | bytes 110600 | tf_op jit(solution)/shard_map/ppermute | solution.py:461
  74.7 23.2 %collective-permute-start.17 = (f32[72,128]{1,0:T(8,128)S(1)}, f32[72,128]{1,0:T(8,128)S(1)}, u32[]{:S(2)}, u32[]{:S(2)}) collective-permute-start(f32[72,128]{1,0:T(8,128)S(1)} %get-tuple-element.70), channel_id=1, source_target_pairs={{0,24},{8,0},{16,8},{24,16},{1,25},{9,1},{17,9},{25,17},{2,26},{10... | collective-permute-start | bytes 110600 | tf_op jit(solution)/shard_map/ppermute | solution.py:461
  78.5 6.6 %collective-permute-start.20 = (f32[8,128]{1,0:T(8,128)S(1)}, f32[8,128]{1,0:T(8,128)S(1)}, u32[]{:S(2)}, u32[]{:S(2)}) collective-permute-start(f32[8,128]{1,0:T(8,128)S(1)} %get-tuple-element.73), channel_id=1, source_target_pairs={{0,9},{1,10},{2,11},{3,12},{4,13},{5,14},{6,15},{7,8},{8,17},{9,18... | collective-permute-start | bytes 12296 | tf_op jit(solution)/shard_map/ppermute | solution.py:461
  85.1 4.8 %collective-permute-start.21 = (f32[8,128]{1,0:T(8,128)S(1)}, f32[8,128]{1,0:T(8,128)S(1)}, u32[]{:S(2)}, u32[]{:S(2)}) collective-permute-start(f32[8,128]{1,0:T(8,128)S(1)} %get-tuple-element.74), channel_id=1, source_target_pairs={{0,15},{1,8},{2,9},{3,10},{4,11},{5,12},{6,13},{7,14},{8,23},{9,16... | collective-permute-start | bytes 12296 | tf_op jit(solution)/shard_map/ppermute | solution.py:461
  90.0 4.8 %collective-permute-start.22 = (f32[8,128]{1,0:T(8,128)S(1)}, f32[8,128]{1,0:T(8,128)S(1)}, u32[]{:S(2)}, u32[]{:S(2)}) collective-permute-start(f32[8,128]{1,0:T(8,128)S(1)} %get-tuple-element.75), channel_id=1, source_target_pairs={{0,25},{1,26},{2,27},{3,28},{4,29},{5,30},{6,31},{7,24},{8,1},{9,2... | collective-permute-start | bytes 12296 | tf_op jit(solution)/shard_map/ppermute | solution.py:461
  94.8 3.0 %collective-permute-start.23 = (f32[8,128]{1,0:T(8,128)S(1)}, f32[8,128]{1,0:T(8,128)S(1)}, u32[]{:S(2)}, u32[]{:S(2)}) collective-permute-start(f32[8,128]{1,0:T(8,128)S(1)} %get-tuple-element.76), channel_id=1, source_target_pairs={{0,31},{1,24},{2,25},{3,26},{4,27},{5,28},{6,29},{7,30},{8,7},{9,0... | collective-permute-start | bytes 12296 | tf_op jit(solution)/shard_map/ppermute | solution.py:461
  102.8 25.9 %collective-permute-start.26 = (f32[160,128]{1,0:T(8,128)S(1)}, f32[160,128]{1,0:T(8,128)S(1)}, u32[]{:S(2)}, u32[]{:S(2)}) collective-permute-start(f32[160,128]{1,0:T(8,128)S(1)} %get-tuple-element.82), channel_id=1, source_target_pairs={{0,1},{1,2},{2,3},{3,4},{4,5},{5,6},{6,7},{7,0},{8,9},{9,10},{10,1... | collective-permute-start | bytes 245768 | tf_op jit(solution)/shard_map/ppermute | solution.py:461
  102.9 25.8 %collective-permute-start.27 = (f32[160,128]{1,0:T(8,128)S(1)}, f32[160,128]{1,0:T(8,128)S(1)}, u32[]{:S(2)}, u32[]{:S(2)}) collective-permute-start(f32[160,128]{1,0:T(8,128)S(1)} %get-tuple-element.83), channel_id=1, source_target_pairs={{0,7},{1,0},{2,1},{3,2},{4,3},{5,4},{6,5},{7,6},{8,15},{9,8},{10,9... | collective-permute-start | bytes 245768 | tf_op jit(solution)/shard_map/ppermute | solution.py:461
  105.5 23.2 %collective-permute-start.24 = (f32[72,128]{1,0:T(8,128)S(1)}, f32[72,128]{1,0:T(8,128)S(1)}, u32[]{:S(2)}, u32[]{:S(2)}) collective-permute-start(f32[72,128]{1,0:T(8,128)S(1)} %get-tuple-element.80), channel_id=1, source_target_pairs={{0,8},{8,16},{16,24},{24,0},{1,9},{9,17},{17,25},{25,1},{2,10},{10... | collective-permute-start | bytes 110600 | tf_op jit(solution)/shard_map/ppermute | solution.py:461
  105.5 23.2 %collective-permute-start.25 = (f32[72,128]{1,0:T(8,128)S(1)}, f32[72,128]{1,0:T(8,128)S(1)}, u32[]{:S(2)}, u32[]{:S(2)}) collective-permute-start(f32[72,128]{1,0:T(8,128)S(1)} %get-tuple-element.81), channel_id=1, source_target_pairs={{0,24},{8,0},{16,8},{24,16},{1,25},{9,1},{17,9},{25,17},{2,26},{10... | collective-permute-start | bytes 110600 | tf_op jit(solution)/shard_map/ppermute | solution.py:461
  109.4 6.6 %collective-permute-start.28 = (f32[8,128]{1,0:T(8,128)S(1)}, f32[8,128]{1,0:T(8,128)S(1)}, u32[]{:S(2)}, u32[]{:S(2)}) collective-permute-start(f32[8,128]{1,0:T(8,128)S(1)} %get-tuple-element.84), channel_id=1, source_target_pairs={{0,9},{1,10},{2,11},{3,12},{4,13},{5,14},{6,15},{7,8},{8,17},{9,18... | collective-permute-start | bytes 12296 | tf_op jit(solution)/shard_map/ppermute | solution.py:461
  116.0 4.8 %collective-permute-start.29 = (f32[8,128]{1,0:T(8,128)S(1)}, f32[8,128]{1,0:T(8,128)S(1)}, u32[]{:S(2)}, u32[]{:S(2)}) collective-permute-start(f32[8,128]{1,0:T(8,128)S(1)} %get-tuple-element.85), channel_id=1, source_target_pairs={{0,15},{1,8},{2,9},{3,10},{4,11},{5,12},{6,13},{7,14},{8,23},{9,16... | collective-permute-start | bytes 12296 | tf_op jit(solution)/shard_map/ppermute | solution.py:461
  120.8 4.8 %collective-permute-start.30 = (f32[8,128]{1,0:T(8,128)S(1)}, f32[8,128]{1,0:T(8,128)S(1)}, u32[]{:S(2)}, u32[]{:S(2)}) collective-permute-start(f32[8,128]{1,0:T(8,128)S(1)} %get-tuple-element.86), channel_id=1, source_target_pairs={{0,25},{1,26},{2,27},{3,28},{4,29},{5,30},{6,31},{7,24},{8,1},{9,2... | collective-permute-start | bytes 12296 | tf_op jit(solution)/shard_map/ppermute | solution.py:461
  125.7 3.0 %collective-permute-start.31 = (f32[8,128]{1,0:T(8,128)S(1)}, f32[8,128]{1,0:T(8,128)S(1)}, u32[]{:S(2)}, u32[]{:S(2)}) collective-permute-start(f32[8,128]{1,0:T(8,128)S(1)} %get-tuple-element.87), channel_id=1, source_target_pairs={{0,31},{1,24},{2,25},{3,26},{4,27},{5,28},{6,29},{7,30},{8,7},{9,0... | collective-permute-start | bytes 12296 | tf_op jit(solution)/shard_map/ppermute | solution.py:461
  134.6 3.4 %collective-permute-start.38 = (f32[8,128]{1,0:T(8,128)S(1)}, f32[8,128]{1,0:T(8,128)S(1)}, u32[]{:S(2)}, u32[]{:S(2)}) collective-permute-start(f32[8,128]{1,0:T(8,128)S(1)} %get-tuple-element.90), channel_id=1, source_target_pairs={{0,7},{1,0},{2,1},{3,2},{4,3},{5,4},{6,5},{7,6},{8,15},{9,8},{10,9... | collective-permute-start | bytes 12296 | tf_op jit(solution)/shard_map/ppermute | solution.py:471
  134.6 6.2 %collective-permute-start.37 = (f32[8,128]{1,0:T(8,128)S(1)}, f32[8,128]{1,0:T(8,128)S(1)}, u32[]{:S(2)}, u32[]{:S(2)}) collective-permute-start(f32[8,128]{1,0:T(8,128)S(1)} %get-tuple-element.90), channel_id=1, source_target_pairs={{0,6},{1,7},{2,0},{3,1},{4,2},{5,3},{6,4},{7,5},{8,14},{9,15},{10,... | collective-permute-start | bytes 12296 | tf_op jit(solution)/shard_map/ppermute | solution.py:471
  135.6 5.2 %collective-permute-start.36 = (f32[8,128]{1,0:T(8,128)S(1)}, f32[8,128]{1,0:T(8,128)S(1)}, u32[]{:S(2)}, u32[]{:S(2)}) collective-permute-start(f32[8,128]{1,0:T(8,128)S(1)} %get-tuple-element.90), channel_id=1, source_target_pairs={{0,5},{1,6},{2,7},{3,0},{4,1},{5,2},{6,3},{7,4},{8,13},{9,14},{10,... | collective-permute-start | bytes 12296 | tf_op jit(solution)/shard_map/ppermute | solution.py:471
  136.4 4.4 %collective-permute-start.35 = (f32[8,128]{1,0:T(8,128)S(1)}, f32[8,128]{1,0:T(8,128)S(1)}, u32[]{:S(2)}, u32[]{:S(2)}) collective-permute-start(f32[8,128]{1,0:T(8,128)S(1)} %get-tuple-element.90), channel_id=1, source_target_pairs={{0,4},{1,5},{2,6},{3,7},{4,0},{5,1},{6,2},{7,3},{8,12},{9,13},{10,... | collective-permute-start | bytes 12296 | tf_op jit(solution)/shard_map/ppermute | solution.py:471
  137.4 3.4 %collective-permute-start.34 = (f32[8,128]{1,0:T(8,128)S(1)}, f32[8,128]{1,0:T(8,128)S(1)}, u32[]{:S(2)}, u32[]{:S(2)}) collective-permute-start(f32[8,128]{1,0:T(8,128)S(1)} %get-tuple-element.90), channel_id=1, source_target_pairs={{0,3},{1,4},{2,5},{3,6},{4,7},{5,0},{6,1},{7,2},{8,11},{9,12},{10,... | collective-permute-start | bytes 12296 | tf_op jit(solution)/shard_map/ppermute | solution.py:471
  138.0 4.5 %collective-permute-start.33 = (f32[8,128]{1,0:T(8,128)S(1)}, f32[8,128]{1,0:T(8,128)S(1)}, u32[]{:S(2)}, u32[]{:S(2)}) collective-permute-start(f32[8,128]{1,0:T(8,128)S(1)} %get-tuple-element.90), channel_id=1, source_target_pairs={{0,2},{1,3},{2,4},{3,5},{4,6},{5,7},{6,0},{7,1},{8,10},{9,11},{10,... | collective-permute-start | bytes 12296 | tf_op jit(solution)/shard_map/ppermute | solution.py:471
  140.8 3.9 %collective-permute-start.32 = (f32[8,128]{1,0:T(8,128)S(1)}, f32[8,128]{1,0:T(8,128)S(1)}, u32[]{:S(2)}, u32[]{:S(2)}) collective-permute-start(f32[8,128]{1,0:T(8,128)S(1)} %get-tuple-element.90), channel_id=1, source_target_pairs={{0,1},{1,2},{2,3},{3,4},{4,5},{5,6},{6,7},{7,0},{8,9},{9,10},{10,1... | collective-permute-start | bytes 12296 | tf_op jit(solution)/shard_map/ppermute | solution.py:471
  144.7 5.5 %collective-permute-start.41 = (f32[8,128]{1,0:T(8,128)S(1)}, f32[8,128]{1,0:T(8,128)S(1)}, u32[]{:S(2)}, u32[]{:S(2)}) collective-permute-start(f32[8,128]{1,0:T(8,128)S(1)} %maximum_maximum_fusion.1), channel_id=1, source_target_pairs={{0,24},{8,0},{16,8},{24,16},{1,25},{9,1},{17,9},{25,17},{2,26},{10... | collective-permute-start | bytes 12296 | tf_op jit(solution)/shard_map/ppermute | solution.py:471
  148.9 4.5 %collective-permute-start.40 = (f32[8,128]{1,0:T(8,128)S(1)}, f32[8,128]{1,0:T(8,128)S(1)}, u32[]{:S(2)}, u32[]{:S(2)}) collective-permute-start(f32[8,128]{1,0:T(8,128)S(1)} %maximum_maximum_fusion.1), channel_id=1, source_target_pairs={{0,16},{8,24},{16,0},{24,8},{1,17},{9,25},{17,1},{25,9},{2,18},{10... | collective-permute-start | bytes 12296 | tf_op jit(solution)/shard_map/ppermute | solution.py:471
  148.9 5.4 %collective-permute-start.39 = (f32[8,128]{1,0:T(8,128)S(1)}, f32[8,128]{1,0:T(8,128)S(1)}, u32[]{:S(2)}, u32[]{:S(2)}) collective-permute-start(f32[8,128]{1,0:T(8,128)S(1)} %maximum_maximum_fusion.1), channel_id=1, source_target_pairs={{0,8},{8,16},{16,24},{24,0},{1,9},{9,17},{17,25},{25,1},{2,10},{10... | collective-permute-start | bytes 12296 | tf_op jit(solution)/shard_map/ppermute | solution.py:471

commit v2 on v1

v2 whole, which is shorter than its diff:
```python
import functools

import jax
import jax.numpy as jnp
from jax import lax
from jax.experimental import pallas as pl
from jax.experimental.pallas import tpu as pltpu
from jax.sharding import PartitionSpec as P

NZ = 64
RELAX = 0.8
PUSH = 0.2
EPS = 1e-06
LANES = 128
VELOCITY = [(a, b, c) for a in (-1, 0, 1) for b in (-1, 0, 1) for c in (-1, 0, 1)]
INDEX = {v: i for i, v in enumerate(VELOCITY)}
WEIGHT = [
    [8.0 / 27, 2.0 / 27, 1.0 / 54, 1.0 / 216][abs(v[0]) + abs(v[1]) + abs(v[2])]
    for v in VELOCITY
]
NORM = [abs(v[0]) + abs(v[1]) + abs(v[2]) for v in VELOCITY]
F32 = jnp.float32
VMEM_LIMIT = 20 * 1024 * 1024


class Grid:
    def __init__(self, rows, width):
        self.rows = rows
        self.cols = width // LANES
        self.tiles = rows // 8
        self.panel = rows + 16
        self.halo = self.cols + 1
        self.local = self.cols * self.tiles
        self.extended = self.halo * self.tiles + 3

    def at(self, i, k, r):
        return (i * (self.cols + 2) + k) * self.panel + 8 + r

    def padded(self, fields):
        return (fields * (self.cols + 2) * self.panel + 8, LANES)


def velocity(i, sign):
    return tuple(sign * n for n in VELOCITY[i]) if i < 27 else (0, 0, 0)


def moving(fields, sign, axis, side):
    return [i for i in range(fields) if velocity(i, sign)[axis] == side]


def lane_masks():
    lane = lax.broadcasted_iota(jnp.int32, (8, LANES), 1)
    return lane >= NZ, lane % NZ == 0, lane % NZ == NZ - 1


def shift_lanes(here, d, masks):
    first, last = masks[1:]
    dy, dz = d[1:]
    if dz == 0:
        return here if dy == 0 else pltpu.roll(here, NZ, 1)
    if dz == 1:
        one, other, edge = 1, NZ + 1, first
    else:
        one, other, edge = LANES - 1, NZ - 1, last
    inner, wrapped = (one, other) if dy == 0 else (other, one)
    return jnp.where(edge, pltpu.roll(here, wrapped, 1), pltpu.roll(here, inner, 1))


def pull(load, d, masks):
    high = masks[0]
    here = load(0)
    if d[1] == 1:
        here = jnp.where(high, load(-1), here)
    elif d[1] == -1:
        here = jnp.where(high, here, load(1))
    return shift_lanes(here, d, masks)


def pull_block(g, buf, sign, k, r, masks, fields=27):
    after = jnp.where(k == g.halo, 1, k + 1)
    out = []
    for i in range(fields):
        d = velocity(i, sign)

        def load(n, i=i, d=d):
            panel = {-1: k - 1, 0: k, 1: after}[n]
            return buf[pl.ds(g.at(i, panel, r - d[0]), 8), :]

        out.append(pull(load, d, masks))
    return out


def pull_edge(g, buf, sign, side, masks, fields=27):
    out = []
    for i in range(fields):
        d = velocity(i, sign)
        if side == 1:
            row = g.rows - d[0]
        else:
            row = {1: g.rows, 0: g.rows + 1, -1: 0}[d[0]]

        def load(n, i=i, row=row):
            return buf[pl.ds(g.at(i, 1 + n, row), g.cols, stride=g.panel), :]

        out.append(pull(load, d, masks))
    return out


def moments(f):
    flat = {}
    along_z = None
    for a in (-1, 0, 1):
        for b in (-1, 0, 1):
            lo, mid, hi = (f[INDEX[(a, b, c)]] for c in (-1, 0, 1))
            flat[a, b] = lo + mid + hi
            diff = hi - lo
            along_z = diff if along_z is None else along_z + diff
    line = {}
    along_y = None
    for a in (-1, 0, 1):
        line[a] = flat[a, -1] + flat[a, 0] + flat[a, 1]
        diff = flat[a, 1] - flat[a, -1]
        along_y = diff if along_y is None else along_y + diff
    return line[-1] + line[0] + line[1], line[1] - line[-1], along_y, along_z


def combos(x, y, z):
    plane = {}
    for a in (-1, 0, 1):
        for b in (-1, 0, 1):
            if (a, b) > (0, 0):
                continue
            if a == 0:
                plane[a, b] = -y if b else None
            else:
                plane[a, b] = -x if b == 0 else (-x - y if b < 0 else y - x)
    out = []
    for a, b, c in VELOCITY[:13]:
        base = plane[a, b]
        if base is None:
            out.append(-z)
        else:
            out.append(base if c == 0 else (base - z if c < 0 else base + z))
    return out


def relax(f, rho, wx, wy, wz, damp, push, solid):
    ux, uy, uz = (wx + push) * damp, wy * damp, wz * damp
    base = 1.0 - 1.5 * (ux * ux + uy * uy + uz * uz)
    keep = 1.0 - 1.0 / RELAX
    gain = rho * (1.0 / RELAX)
    level = [gain * w for w in (8.0 / 27, 2.0 / 27, 1.0 / 54, 1.0 / 216)]
    along = combos(3.0 * ux, 3.0 * uy, 3.0 * uz)
    out = [None] * 27
    for i in range(13):
        j = 26 - i
        even = base + 0.5 * (along[i] * along[i])
        lift = level[NORM[i]]
        out[i] = jnp.where(solid, f[j], keep * f[i] + lift * (even + along[i]))
        out[j] = jnp.where(solid, f[i], keep * f[j] + lift * (even - along[i]))
    out[13] = jnp.where(solid, f[13], keep * f[13] + level[0] * base)
    return out


def pulled_moments(p):
    first = {}
    for a in (-1, 0, 1):
        for b in (-1, 0, 1):
            lo, mid, hi = (p[INDEX[(a, b, c)]] for c in (-1, 0, 1))
            both = lo + hi
            first[a, b] = (4.0 * mid + both, hi - lo, both)
    second = {}
    for a in (-1, 0, 1):
        lo, mid, hi = (first[a, b] for b in (-1, 0, 1))
        b0 = lo[0] + hi[0]
        b1 = lo[1] + hi[1]
        second[a] = dict(
            one=4.0 * mid[0] + b0,
            y=hi[0] - lo[0],
            yy=b0,
            z=4.0 * mid[1] + b1,
            yz=hi[1] - lo[1],
            zz=4.0 * mid[2] + lo[2] + hi[2],
        )
    lo, mid, hi = (second[a] for a in (-1, 0, 1))

    def full(key):
        return 4.0 * mid[key] + lo[key] + hi[key]

    xx = lo["one"] + hi["one"]
    return dict(
        one=4.0 * mid["one"] + xx,
        x=hi["one"] - lo["one"],
        xx=xx,
        y=full("y"),
        xy=hi["y"] - lo["y"],
        yy=full("yy"),
        z=full("z"),
        xz=hi["z"] - lo["z"],
        yz=full("yz"),
        zz=full("zz"),
    )


def adjoint_scalars(p, rho, wx, wy, wz, damp, push, solid):
    ux, uy, uz = (wx + push) * damp, wy * damp, wz * damp
    s = pulled_moments(p)
    scale = 1.0 / (216.0 * RELAX)
    one = s["one"] * scale
    b = [s[k] * (3.0 * scale) for k in ("x", "y", "z")]
    d = {k: s[k] * (9.0 * scale) for k in ("xx", "xy", "yy", "xz", "yz", "zz")}
    qx = d["xx"] * ux + d["xy"] * uy + d["xz"] * uz
    qy = d["xy"] * ux + d["yy"] * uy + d["yz"] * uz
    qz = d["xz"] * ux + d["yz"] * uy + d["zz"] * uz
    linear = b[0] * ux + b[1] * uy + b[2] * uz
    square = ux * ux + uy * uy + uz * uz
    even = one + linear + 0.5 * (qx * ux + qy * uy + qz * uz) - 1.5 * one * square
    three = 3.0 * one
    gx = (b[0] + qx - three * ux) * damp
    gy = (b[1] + qy - three * uy) * damp
    gz = (b[2] + qz - three * uz) * damp
    even = even - (gx * wx + gy * wy + gz * wz)
    porous = jnp.where(solid, 0.0, -rho * (gx * ux + gy * uy + gz * uz))
    return even, gx, gy, gz, porous


def adjoint_spread(p, even, gx, gy, gz, solid):
    keep = 1.0 - 1.0 / RELAX
    along = combos(gx, gy, gz)
    out = [None] * 27
    for i in range(13):
        j = 26 - i
        out[i] = jnp.where(solid, p[j], keep * p[i] + (even + along[i]))
        out[j] = jnp.where(solid, p[i], keep * p[j] + (even - along[i]))
    out[13] = jnp.where(solid, p[13], keep * p[13] + even)
    return out


def pack_x(g, buf, sign, fields, up, down):
    for side, ref in ((1, up), (-1, down)):
        edge, inner = (g.rows - 1, g.rows - 2) if side == 1 else (0, 1)
        lines = [(i, r) for i in moving(fields, sign, 0, side) for r in (edge, inner)]
        lines += [(i, edge) for i in moving(fields, sign, 0, 0)]
        for n, (i, r) in enumerate(lines):
            ref[n * g.cols : (n + 1) * g.cols, :] = buf[
                pl.ds(g.at(i, 1, r), g.cols, stride=g.panel), :
            ]


def unpack_x(g, buf, sign, fields, up, down):
    for side, ref in ((1, up), (-1, down)):
        lines = []
        for i in moving(fields, sign, 0, side):
            if side == 1:
                lines += [(i, (-1, g.rows + 1)), (i, (g.rows,))]
            else:
                lines += [(i, (g.rows,)), (i, (g.rows + 1,))]
        for i in moving(fields, sign, 0, 0):
            lines.append((i, (g.rows + 1 if side == 1 else g.rows,)))
        for n, (i, targets) in enumerate(lines):
            value = ref[n * g.cols : (n + 1) * g.cols, :]
            for r in targets:
                buf[pl.ds(g.at(i, 1, r), g.cols, stride=g.panel), :] = value
    for i in moving(fields, sign, 0, -1):
        buf[pl.ds(g.at(i, 1, g.rows + 2), g.cols, stride=g.panel), :] = buf[
            pl.ds(g.at(i, 1, 0), g.cols, stride=g.panel), :
        ]


def slot_rows(g, slots, n):
    pieces = [(n * g.rows + 8 * a, 8 * a, 8) for a in range(g.tiles)]
    return pieces + [(slots * g.rows + 2 * n, g.rows, 2)]


def still_pairs(fields, sign):
    still = moving(fields, sign, 1, 0)
    half = (len(still) + 1) // 2
    return [(still[n], still[n + half] if n + half < len(still) else None) for n in range(half)]


def y_slots(fields, sign):
    return 9 + len(still_pairs(fields, sign))


def pack_y(g, buf, sign, fields, up, down, high):
    slots = y_slots(fields, sign)
    for side, ref in ((1, up), (-1, down)):
        k = g.cols if side == 1 else 1
        for n, i in enumerate(moving(fields, sign, 1, side)):
            for to, r, count in slot_rows(g, slots, n):
                ref[to : to + count, :] = buf[pl.ds(g.at(i, k, r), count), :]
        for n, (i, j) in enumerate(still_pairs(fields, sign)):
            for to, r, count in slot_rows(g, slots, 9 + n):
                value = buf[pl.ds(g.at(i, k, r), count), :]
                if j is not None:
                    other = pltpu.roll(buf[pl.ds(g.at(j, k, r), count), :], NZ, 1)
                    pair = (value, other) if side == 1 else (other, value)
                    value = jnp.where(high[:count], *pair)
                ref[to : to + count, :] = value


def unpack_y(g, buf, sign, fields, up, down, high):
    slots = y_slots(fields, sign)
    for side, ref in ((1, up), (-1, down)):
        for n, i in enumerate(moving(fields, sign, 1, side)):
            for to, r, count in slot_rows(g, slots, n):
                value = ref[to : to + count, :]
                for k in (0, g.halo) if side == 1 else (g.halo,):
                    buf[pl.ds(g.at(i, k, r), count), :] = value
    for n, (i, j) in enumerate(still_pairs(fields, sign)):
        for to, r, count in slot_rows(g, slots, 9 + n):
            before, after = up[to : to + count, :], down[to : to + count, :]
            mask = high[:count]
            buf[pl.ds(g.at(i, g.halo, r), count), :] = jnp.where(mask, before, after)
            if j is not None:
                buf[pl.ds(g.at(j, g.halo, r), count), :] = pltpu.roll(
                    jnp.where(mask, after, before), NZ, 1
                )
    for i in moving(fields, sign, 0, 1):
        for k in (0, g.halo) if velocity(i, sign)[1] == 1 else (g.halo,):
            buf[pl.ds(g.at(i, k, -1), 1), :] = buf[pl.ds(g.at(i, k, g.rows + 1), 1), :]
    for i in moving(fields, sign, 0, -1):
        for k in (0, g.halo) if velocity(i, sign)[1] == 1 else (g.halo,):
            buf[pl.ds(g.at(i, k, g.rows + 2), 1), :] = buf[pl.ds(g.at(i, k, 0), 1), :]


def by_parity(axis, first, second, act):
    even = lax.rem(lax.axis_index(axis), 2) == 0

    @pl.when(even)
    def _():
        act(first, second)

    @pl.when(jnp.logical_not(even))
    def _():
        act(second, first)


def load_fields(ref, tiles, t, count):
    return [ref[pl.ds((n * tiles + t) * 8, 8), :] for n in range(count)]


def save_fields(ref, tiles, t, values):
    for n, value in enumerate(values):
        ref[pl.ds((n * tiles + t) * 8, 8), :] = value


def over_tiles(g, panels, body, before=None, after=None):
    def column(k, carry):
        if before is not None:
            before(k)

        def tile(a, inner):
            body(k, pl.multiple_of(a * 8, 8), (k - 1) * g.tiles + a)
            return inner

        lax.fori_loop(0, g.tiles, tile, 0)
        if after is not None:
            after(k)
        return carry

    lax.fori_loop(1, panels + 1, column, 0)


def over_extended(g, buf, out, sign, fields, masks, compute):
    def body(k, r, t):
        values = compute(pull_block(g, buf, sign, k, r, masks, fields), t)
        for i in range(27):
            out[pl.ds(g.at(i, k, r), 8), :] = values[i]

    over_tiles(g, g.halo, body)
    t = g.halo * g.tiles
    values = compute(pull_block(g, buf, sign, g.halo, g.rows, masks, fields), t)
    for i in range(27):
        dx = velocity(i, sign)[0]
        if dx == -1:
            out[pl.ds(g.at(i, g.halo, g.rows), 1), :] = values[i][0:1]
        elif dx == 1:
            out[pl.ds(g.at(i, g.halo, -1), 1), :] = values[i][1:2]
    for n, side in ((1, 1), (2, -1)):
        values = compute(pull_edge(g, buf, sign, side, masks, fields), t + n)
        for i in moving(27, sign, 0, -side):
            row = g.rows if side == 1 else -1
            out[pl.ds(g.at(i, 1, row), g.cols, stride=g.panel), :] = values[i]
    for i in moving(27, sign, 1, 1):
        for a in range(g.tiles):
            out[pl.ds(g.at(i, 0, 8 * a), 8), :] = out[pl.ds(g.at(i, g.halo, 8 * a), 8), :]
        for r in (-1, g.rows):
            out[pl.ds(g.at(i, 0, r), 1), :] = out[pl.ds(g.at(i, g.halo, r), 1), :]


def block_of(ref, k):
    return ref.at[:, :, pl.ds(pl.multiple_of((k - 1) * LANES, LANES), LANES)]


def first_kernel(g, pops, porosity, solid, labels, out, state, x_first, x_second, stage, sems):
    def copy(k):
        return pltpu.make_async_copy(block_of(pops, k), stage.at[k - 1], sems.at[k - 1])

    for k in range(1, g.cols + 1):
        copy(k).start()

    def body(k, r, t):
        f = [stage[k - 1, i, pl.ds(r, 8), :] for i in range(27)]
        spot = (pl.ds(r, 8), pl.ds(pl.multiple_of((k - 1) * LANES, LANES), LANES))
        wall = solid[spot]
        label = labels[spot]
        damp = 1.0 / (1.0 + porosity[spot])
        push = jnp.where(label == 1, PUSH, jnp.where(label == 2, -PUSH, 0.0))
        rho, mx, my, mz = moments(f)
        inverse = 1.0 / rho
        flow = (rho, mx * inverse, my * inverse, mz * inverse, damp, push)
        extra = (damp, push, wall.astype(F32))
        save_fields(state, g.local, t, flow + extra[2:])
        values = relax(f, *flow, wall == 1)
        for i, value in enumerate(tuple(values) + extra):
            out[pl.ds(g.at(i, k, r), 8), :] = value

    over_tiles(g, g.cols, body, before=lambda k: copy(k).wait())
    by_parity("gx", x_first, x_second, functools.partial(pack_x, g, out, 1, 30))


def relay_kernel(g, sign, fields, padded, x_first, x_second, buf, y_first, y_second):
    del padded
    high = lane_masks()[0]
    by_parity("gx", x_second, x_first, functools.partial(unpack_x, g, buf, sign, fields))
    by_parity(
        "gy",
        y_first,
        y_second,
        lambda up, down: pack_y(g, buf, sign, fields, up, down, high),
    )


def second_kernel(g, padded, y_first, y_second, buf, out, state):
    del padded
    masks = lane_masks()
    by_parity(
        "gy", y_second, y_first, lambda up, down: unpack_y(g, buf, 1, 30, up, down, masks[0])
    )

    def compute(values, t):
        f, (damp, push, wall) = values[:27], values[27:]
        rho, mx, my, mz = moments(f)
        inverse = 1.0 / rho
        flow = (rho, mx * inverse, my * inverse, mz * inverse, damp, push)
        save_fields(state, g.extended, t, flow + (wall,))
        return relax(f, *flow, wall > 0.5)

    over_extended(g, buf, out, 1, 30, masks, compute)


def third_kernel(g, buf, adjoint, final, out, x_first, x_second, stage_out, stage_in, *sems):
    sems_out, sems_in = sems
    masks = lane_masks()

    def copy_in(k):
        return pltpu.make_async_copy(block_of(adjoint, k), stage_in.at[k - 1], sems_in.at[k - 1])

    def copy_out(k):
        return pltpu.make_async_copy(stage_out.at[k - 1], block_of(final, k), sems_out.at[k - 1])

    for k in range(1, g.cols + 1):
        copy_in(k).start()

    def body(k, r, t):
        f = pull_block(g, buf, 1, k, r, masks)
        for i in range(27):
            stage_out[k - 1, i, pl.ds(r, 8), :] = f[i]
        rho, mx, my, mz = moments(f)
        inverse = 1.0 / rho
        wx, wy, wz = mx * inverse, my * inverse, mz * inverse
        even = -(wx * wx + wy * wy + wz * wz) * inverse
        along = combos(wx * inverse, wy * inverse, wz * inverse)
        for i in range(27):
            value = stage_in[k - 1, i, pl.ds(r, 8), :] + even
            if i < 13:
                value = value + along[i]
            elif i > 13:
                value = value - along[26 - i]
            out[pl.ds(g.at(i, k, r), 8), :] = value

    over_tiles(
        g,
        g.cols,
        body,
        before=lambda k: copy_in(k).wait(),
        after=lambda k: copy_out(k).start(),
    )
    by_parity("gx", x_first, x_second, functools.partial(pack_x, g, out, -1, 27))
    for k in range(1, g.cols + 1):
        copy_out(k).wait()


def fourth_kernel(g, padded, state, y_first, y_second, buf, out, total):
    del padded
    masks = lane_masks()
    by_parity(
        "gy", y_second, y_first, lambda up, down: unpack_y(g, buf, -1, 27, up, down, masks[0])
    )

    def compute(p, t):
        *flow, wall = load_fields(state, g.extended, t, 7)
        even, gx, gy, gz, porous = adjoint_scalars(p, *flow, wall > 0.5)
        save_fields(total, g.extended, t, [porous])
        return adjoint_spread(p, even, gx, gy, gz, wall > 0.5)

    over_extended(g, buf, out, -1, 27, masks, compute)


def fifth_kernel(g, buf, state, before, result, total, peak, stage_out, sems_out):
    masks = lane_masks()

    def copy_out(k):
        return pltpu.make_async_copy(stage_out.at[k - 1], block_of(result, k), sems_out.at[k - 1])

    peak[...] = jnp.zeros((8, LANES), F32)

    def body(k, r, t):
        p = pull_block(g, buf, -1, k, r, masks)
        *flow, wall = load_fields(state, g.local, t, 7)
        even, gx, gy, gz, porous = adjoint_scalars(p, *flow, wall > 0.5)
        here = load_fields(before, g.extended, t, 1)[0] + porous
        save_fields(total, g.local, t, [here])
        peak[...] = jnp.maximum(peak[...], jnp.abs(here))
        for i, value in enumerate(adjoint_spread(p, even, gx, gy, gz, wall > 0.5)):
            stage_out[k - 1, i, pl.ds(r, 8), :] = value

    over_tiles(g, g.cols, body, after=lambda k: copy_out(k).start())
    for k in range(1, g.cols + 1):
        copy_out(k).wait()


def scale_kernel(g, total, peak, out):
    largest = jnp.max(peak[...])
    factor = 1.0 / (jnp.full((8, LANES), largest, F32) + EPS)
    for c in range(g.cols):
        for a in range(g.tiles):
            value = load_fields(total, g.local, c * g.tiles + a, 1)[0] * factor
            out[8 * a : 8 * a + 8, c * LANES : (c + 1) * LANES] = value


def swap_pairs(count, start):
    pairs = []
    for i in range(start, count, 2):
        j = (i + 1) % count
        pairs += [(i, j), (j, i)]
    return pairs


def swap(axis, count, first, second):
    return (
        lax.ppermute(first, axis, swap_pairs(count, 0)),
        lax.ppermute(second, axis, swap_pairs(count, 1)),
    )


def largest_of_all(peak, sizes):
    for axis, count in (("gy", sizes[1]), ("gx", sizes[0])):
        step = 1
        while step < count:
            other = lax.ppermute(peak, axis, [(i, i ^ step) for i in range(count)])
            peak = jnp.maximum(peak, other)
            step *= 2
    return peak


def on_device(sizes, populations, adjoint_in, porosity, solid, labels):
    rows, width = porosity.shape
    g = Grid(rows, width)
    in_vmem = pl.BlockSpec(memory_space=pltpu.VMEM)
    anywhere = pl.BlockSpec(memory_space=pl.ANY)
    hbm = pl.BlockSpec(memory_space=pltpu.HBM)
    nx, ny = sizes

    def vmem(*shape):
        return pltpu.VMEM(shape, F32)

    def fields(count, tiles):
        return vmem(count * tiles * 8, LANES)

    def padded(count):
        return vmem(*g.padded(count))

    def x_parcels(count):
        return [vmem((count) * g.cols, LANES)] * 2

    def y_parcels(count, sign):
        slots = y_slots(count, sign)
        return [vmem(-(-slots * (rows + 2) // 8) * 8, LANES)] * 2

    whole = jax.ShapeDtypeStruct(populations.shape, F32)
    stage = pltpu.VMEM((g.cols, 27, rows, LANES), F32)
    sems = pltpu.SemaphoreType.DMA((g.cols,))

    def call(name, kernel, in_specs, out_shape, out_specs, scratch=(), aliases=None):
        return pl.pallas_call(
            functools.partial(kernel, g),
            in_specs=in_specs,
            out_shape=out_shape,
            out_specs=out_specs,
            scratch_shapes=list(scratch),
            input_output_aliases=aliases or {},
            compiler_params=pltpu.CompilerParams(vmem_limit_bytes=VMEM_LIMIT),
            name=name,
        )

    def pin(x):
        return pltpu.with_memory_space_constraint(x, pltpu.VMEM)

    def exchange(buf, parcels, sign, count):
        parcels = swap("gx", nx, *parcels)
        buf, *parcels = call(
            "relay",
            lambda grid, *refs: relay_kernel(grid, sign, count, *refs),
            [in_vmem] * 3,
            [padded(count)] + y_parcels(count, sign),
            [in_vmem] * 3,
            aliases={0: 0},
        )(pin(buf), *parcels)
        return buf, swap("gy", ny, *parcels)

    post, state0, *parcels = call(
        "collide_first",
        first_kernel,
        [anywhere, in_vmem, in_vmem, in_vmem],
        [padded(30), fields(7, g.local)] + x_parcels(30),
        [in_vmem] * 4,
        [stage, sems],
    )(populations, porosity, solid, labels)
    post, parcels = exchange(post, parcels, 1, 30)

    _, post, state1 = call(
        "collide_second",
        second_kernel,
        [in_vmem] * 3,
        [padded(30), padded(27), fields(7, g.extended)],
        [in_vmem] * 3,
        aliases={0: 0},
    )(pin(post), *parcels)

    final, field, *parcels = call(
        "stream_and_seed",
        third_kernel,
        [in_vmem, anywhere],
        [whole, padded(27)] + x_parcels(27),
        [hbm] + [in_vmem] * 3,
        [stage, stage, sems, sems],
    )(pin(post), adjoint_in)
    field, parcels = exchange(field, parcels, -1, 27)

    _, field, total = call(
        "adjoint_second",
        fourth_kernel,
        [in_vmem] * 4,
        [padded(27), padded(27), fields(1, g.extended)],
        [in_vmem] * 3,
        aliases={0: 0},
    )(pin(field), pin(state1), *parcels)

    adjoint_out, total, peak = call(
        "adjoint_first",
        fifth_kernel,
        [in_vmem] * 3,
        [whole, fields(1, g.local), vmem(8, LANES)],
        [hbm] + [in_vmem] * 2,
        [stage, sems],
    )(pin(field), pin(state0), pin(total))

    sensitivity = call(
        "normalize",
        scale_kernel,
        [in_vmem, in_vmem],
        jax.ShapeDtypeStruct(porosity.shape, F32),
        in_vmem,
    )(pin(total), largest_of_all(peak, sizes))
    return final, adjoint_out, sensitivity


def solution(mesh):
    sizes = (mesh.shape["gx"], mesh.shape["gy"])
    whole, flat = P(None, "gx", "gy"), P("gx", "gy")
    return jax.shard_map(
        functools.partial(on_device, sizes),
        mesh=mesh,
        in_specs=(whole, whole, flat, flat, flat),
        out_specs=(whole, whole, flat),
        check_vma=False,
    )
```

time: 155 us -> 87.5 us (0.56)
  waiting for transfers between devices: 85.7 us -> 39.1 us
  starting transfers between devices: 38.6 us -> 15.4 us
  Pallas kernels: 25.2 us -> 27.3 us
    ppermute x42 -> x13, waiting for transfers between devices: 85.7 us -> 39.1 us  [the longest x4 21.8 us: swap(): lax.ppermute(second, axis, swap_pairs(count, 1))]
    ppermute x42 -> x13, starting transfers between devices: 38.6 us -> 15.4 us  [the longest x4 9.6 us: swap(): lax.ppermute(second, axis, swap_pairs(count, 1))]
    pallas_call x6 -> x8, Pallas kernels: 25.2 us -> 27.3 us  [the longest x1 6.08 us: on_device(): call('stream_and_seed', third_kernel, [in_vmem, anywhere], [whole, padded...]
  transfers between devices with their start and end apart: 42 -> 13, of which waited for: 21 -> 11; matrix products, arithmetic and copies ran while one was open for 0% -> 0% of each run, Pallas kernels for 0% -> 0%
where the time goes in v2:
time: 87.5 us; the launch traced here: 87.3 us
  waiting for transfers between devices  39.1 us (45%)
  Pallas kernels  27.3 us (31%)
  starting transfers between devices  15.4 us (18%)
  local copies, waits for them, and re-layouts  4.71 us (5%)
    ppermute x4, waiting for transfers between devices, swap(): lax.ppermute(second, axis, swap_pairs(count, 1))  21.8 us
    ppermute x5, waiting for transfers between devices, largest_of_all(): other = lax.ppermute(peak, axis, [(i, i ^ step) for i in range(count)])  14.6 us
    ppermute x4, starting transfers between devices, swap(): lax.ppermute(second, axis, swap_pairs(count, 1))  9.6 us
    pallas_call x1, Pallas kernels, on_device(): call('stream_and_seed', third_kernel, [in_vmem, anywhere], [whole, padded...  6.08 us
    pallas_call x1, Pallas kernels, on_device(): call('collide_second', second_kernel, [in_vmem] * 3, [padded(30), padded(...  6.06 us
    pallas_call x1, Pallas kernels, on_device(): call('adjoint_second', fourth_kernel, [in_vmem] * 4, [padded(27), padded(...  5.73 us
    pallas_call x1, Pallas kernels, on_device(): call('adjoint_first', fifth_kernel, [in_vmem] * 3, [whole, fields(1, g.lo...  5.62 us
    unnamed x10, local copies, waits for them, and re-layouts  4.71 us
  transfers between devices with their start and end apart: 13, of which 11 were waited for; matrix products, arithmetic and copies ran while one was open for 0% of the time, Pallas kernels for 0%

profile of v2, /device:TPU:0, one launch (start us, length us, event | category | flops | bytes accessed | tf_op | source)
XLA Modules:
  0.0 87.3 jit_solution(10272021789352833452)
XLA Ops:
  0.6 0.0 copy-start.1
  0.6 2.0 %copy-done.1 = f32[27,32,1024]{2,1,0:T(8,128)S(1)} copy-done((f32[27,32,1024]{2,1,0:T(8,128)S(1)}, f32[27,32,1024]{2,1,0:T(8,128)}, u32[]{:S(2)}) %copy-start.1) | copy-done | bytes 3538968
  2.6 0.0 copy-start.2
  2.6 0.9 %copy-done.2 = f32[32,1024]{1,0:T(8,128)S(1)} copy-done((f32[32,1024]{1,0:T(8,128)S(1)}, f32[32,1024]{1,0:T(8,128)}, u32[]{:S(2)}) %copy-start.2) | copy-done | bytes 131096
  3.5 0.0 copy-start.3
  3.5 0.9 %copy-done.3 = s32[32,1024]{1,0:T(8,128)S(1)} copy-done((s32[32,1024]{1,0:T(8,128)S(1)}, s32[32,1024]{1,0:T(8,128)}, u32[]{:S(2)}) %copy-start.3) | copy-done | bytes 131096
  4.4 0.0 copy-start.4
  4.4 0.9 %copy-done.4 = s32[32,1024]{1,0:T(8,128)S(1)} copy-done((s32[32,1024]{1,0:T(8,128)S(1)}, s32[32,1024]{1,0:T(8,128)}, u32[]{:S(2)}) %copy-start.4) | copy-done | bytes 131096
  5.3 2.5 %collide_first.1 = (f32[14408,128]{1,0:T(8,128)S(1)}, f32[1792,128]{1,0:T(8,128)S(1)}, f32[240,128]{1,0:T(8,128)S(1)}, f32[240,128]{1,0:T(8,128)S(1)}) custom-call(f32[27,32,1024]{2,1,0:T(8,128)S(1)} %copy-done.1, f32[32,1024]{1,0:T(8,128)S(1)} %copy-done.2, s32[32,1024]{1,0:T(8,128)S(1)} %copy-done.3, s32[32,1024]{1,0:T(8,128)S(1)} %copy-done.4), custom_call_target="tpu_custom_call" | custom-call | tf_op jit(solution)/shard_map/collide_first/pallas_call | solution.py:623
  7.9 3.1 %collective-permute-start = (f32[240,128]{1,0:T(8,128)S(1)}, f32[240,128]{1,0:T(8,128)S(1)}, u32[]{:S(2)}, u32[]{:S(2)}) collective-permute-start(f32[240,128]{1,0:T(8,128)S(1)} %get-tuple-element.25), channel_id=1, source_target_pairs={{0,8},{8,0},{16,24},{24,16},{1,9},{9,1},{17,25},{25,17},{2,10},{10... | collective-permute-start | bytes 368648 | tf_op jit(solution)/shard_map/ppermute | solution.py:553
  11.0 2.5 %collective-permute-start.1 = (f32[240,128]{1,0:T(8,128)S(1)}, f32[240,128]{1,0:T(8,128)S(1)}, u32[]{:S(2)}, u32[]{:S(2)}) collective-permute-start(f32[240,128]{1,0:T(8,128)S(1)} %get-tuple-element.26), channel_id=1, source_target_pairs={{8,16},{16,8},{24,0},{0,24},{9,17},{17,9},{25,1},{1,25},{10,18},{1... | collective-permute-start | bytes 368648 | tf_op jit(solution)/shard_map/ppermute | solution.py:554
  13.4 0.8 collective-permute-done.refs_1_
  14.3 4.9 %collective-permute-done.1.refs_2_ = f32[240,128]{1,0:T(8,128)S(1)} collective-permute-done((f32[240,128]{1,0:T(8,128)S(1)}, f32[240,128]{1,0:T(8,128)S(1)}, u32[]{:S(2)}, u32[]{:S(2)}) %collective-permute-start.1) | collective-permute-done | bytes 122912 | tf_op jit(solution)/shard_map/ppermute | solution.py:554
  19.2 0.0 copy-start
  19.2 0.3 relay.2
  19.5 0.1 collective-permute-start.2
  19.6 2.5 %collective-permute-start.3 = (f32[512,128]{1,0:T(8,128)S(1)}, f32[512,128]{1,0:T(8,128)S(1)}, u32[]{:S(2)}, u32[]{:S(2)}) collective-permute-start(f32[512,128]{1,0:T(8,128)S(1)} %get-tuple-element.29), channel_id=1, source_target_pairs={{1,2},{2,1},{3,4},{4,3},{5,6},{6,5},{7,0},{0,7},{9,10},{10,9},{11,... | collective-permute-start | bytes 786440 | tf_op jit(solution)/shard_map/ppermute | solution.py:554
  22.1 0.0 collective-permute-done.2.y_first
  22.1 6.4 %collective-permute-done.3.y_second = f32[512,128]{1,0:T(8,128)S(1)} collective-permute-done((f32[512,128]{1,0:T(8,128)S(1)}, f32[512,128]{1,0:T(8,128)S(1)}, u32[]{:S(2)}, u32[]{:S(2)}) %collective-permute-start.3) | collective-permute-done | bytes 262176 | tf_op jit(solution)/shard_map/ppermute | solution.py:554
  28.5 6.1 %collide_second.1 = (f32[14408,128]{1,0:T(8,128)S(1)}, f32[12968,128]{1,0:T(8,128)S(1)}, f32[2184,128]{1,0:T(8,128)S(1)}) custom-call(f32[14408,128]{1,0:T(8,128)S(1)} %get-tuple-element.27.padded, f32[512,128]{1,0:T(8,128)S(1)} %collective-permute-done.2.y_first, f32[512,128]{1,0:T(8,128)S(1)} %collective-permute-done.3.y_second), custom_call_target="tpu_custom_call", output_to_operand_aliasing={{0}: (0, {})} | custom-call | tf_op jit(solution)/shard_map/collide_second/pallas_call | solution.py:633
  34.6 0.0 copy-done
  34.6 6.1 %stream_and_seed.1 = (f32[27,32,1024]{2,1,0:T(8,128)}, f32[12968,128]{1,0:T(8,128)S(1)}, f32[216,128]{1,0:T(8,128)S(1)}, f32[216,128]{1,0:T(8,128)S(1)}) custom-call(f32[12968,128]{1,0:T(8,128)S(1)} %get-tuple-element.30.buf, f32[27,32,1024]{2,1,0:T(8,128)S(1)} %copy-done), custom_call_target="tpu_custom_call" | custom-call | tf_op jit(solution)/shard_map/stream_and_seed/pallas_call | solution.py:642
  40.7 0.6 collective-permute-start.4
  41.3 2.6 %collective-permute-start.5 = (f32[216,128]{1,0:T(8,128)S(1)}, f32[216,128]{1,0:T(8,128)S(1)}, u32[]{:S(2)}, u32[]{:S(2)}) collective-permute-start(f32[216,128]{1,0:T(8,128)S(1)} %get-tuple-element.34), channel_id=1, source_target_pairs={{8,16},{16,8},{24,0},{0,24},{9,17},{17,9},{25,1},{1,25},{10,18},{1... | collective-permute-start | bytes 331784 | tf_op jit(solution)/shard_map/ppermute | solution.py:554
  44.0 1.8 %collective-permute-done.4.refs_1_ = f32[216,128]{1,0:T(8,128)S(1)} collective-permute-done((f32[216,128]{1,0:T(8,128)S(1)}, f32[216,128]{1,0:T(8,128)S(1)}, u32[]{:S(2)}, u32[]{:S(2)}) %collective-permute-start.4) | collective-permute-done | bytes 110624 | tf_op jit(solution)/shard_map/ppermute | solution.py:553
  45.8 3.6 %collective-permute-done.5.refs_2_ = f32[216,128]{1,0:T(8,128)S(1)} collective-permute-done((f32[216,128]{1,0:T(8,128)S(1)}, f32[216,128]{1,0:T(8,128)S(1)}, u32[]{:S(2)}, u32[]{:S(2)}) %collective-permute-start.5) | collective-permute-done | bytes 110624 | tf_op jit(solution)/shard_map/ppermute | solution.py:554
  49.4 0.2 relay.3
  49.6 0.1 collective-permute-start.6
  49.7 1.9 %collective-permute-start.7 = (f32[480,128]{1,0:T(8,128)S(1)}, f32[480,128]{1,0:T(8,128)S(1)}, u32[]{:S(2)}, u32[]{:S(2)}) collective-permute-start(f32[480,128]{1,0:T(8,128)S(1)} %get-tuple-element.38), channel_id=1, source_target_pairs={{1,2},{2,1},{3,4},{4,3},{5,6},{6,5},{7,0},{0,7},{9,10},{10,9},{11,... | collective-permute-start | bytes 737288 | tf_op jit(solution)/shard_map/ppermute | solution.py:554
  51.6 0.0 collective-permute-done.6.y_first
  51.6 6.9 %collective-permute-done.7.y_second = f32[480,128]{1,0:T(8,128)S(1)} collective-permute-done((f32[480,128]{1,0:T(8,128)S(1)}, f32[480,128]{1,0:T(8,128)S(1)}, u32[]{:S(2)}, u32[]{:S(2)}) %collective-permute-start.7) | collective-permute-done | bytes 245792 | tf_op jit(solution)/shard_map/ppermute | solution.py:554
  58.5 5.7 %adjoint_second.1 = (f32[12968,128]{1,0:T(8,128)S(1)}, f32[12968,128]{1,0:T(8,128)S(1)}, f32[312,128]{1,0:T(8,128)S(1)}) custom-call(f32[12968,128]{1,0:T(8,128)S(1)} %get-tuple-element.35.padded, f32[2184,128]{1,0:T(8,128)S(1)} %get-tuple-element.36.state, f32[480,128]{1,0:T(8,128)S(1)} %collective-permute-done.6.y_first, ...), custom_call_target="tpu_custom_call", output_to_operand_aliasing={{0}: (0, {})} | custom-call | tf_op jit(solution)/shard_map/adjoint_second/pallas_call | solution.py:652
  64.3 5.6 %adjoint_first.1 = (f32[27,32,1024]{2,1,0:T(8,128)}, f32[256,128]{1,0:T(8,128)S(1)}, f32[8,128]{1,0:T(8,128)S(1)}) custom-call(f32[12968,128]{1,0:T(8,128)S(1)} %get-tuple-element.39.buf, f32[1792,128]{1,0:T(8,128)S(1)} %get-tuple-element.40.state, f32[312,128]{1,0:T(8,128)S(1)} %get-tuple-element.41.before), custom_call_target="tpu_custom_call" | custom-call | tf_op jit(solution)/shard_map/adjoint_first/pallas_call | solution.py:661
  69.9 0.1 collective-permute-start.8
  70.0 1.1 %collective-permute-done.8 = f32[8,128]{1,0:T(8,128)S(1)} collective-permute-done((f32[8,128]{1,0:T(8,128)S(1)}, f32[8,128]{1,0:T(8,128)S(1)}, u32[]{:S(2)}, u32[]{:S(2)}) %collective-permute-start.8) | collective-permute-done | bytes 4128 | tf_op jit(solution)/shard_map/ppermute | solution.py:562
  71.1 0.0 collective-permute-start.9
  71.1 3.6 %collective-permute-done.9 = f32[8,128]{1,0:T(8,128)S(1)} collective-permute-done((f32[8,128]{1,0:T(8,128)S(1)}, f32[8,128]{1,0:T(8,128)S(1)}, u32[]{:S(2)}, u32[]{:S(2)}) %collective-permute-start.9) | collective-permute-done | bytes 4128 | tf_op jit(solution)/shard_map/ppermute | solution.py:562
  74.7 1.6 %collective-permute-start.10 = (f32[8,128]{1,0:T(8,128)S(1)}, f32[8,128]{1,0:T(8,128)S(1)}, u32[]{:S(2)}, u32[]{:S(2)}) collective-permute-start(f32[8,128]{1,0:T(8,128)S(1)} %max.16), channel_id=1, source_target_pairs={{0,4},{1,5},{2,6},{3,7},{4,0},{5,1},{6,2},{7,3},{8,12},{9,13},{10,... | collective-permute-start | bytes 12296 | tf_op jit(solution)/shard_map/ppermute | solution.py:562
  76.3 2.1 %collective-permute-done.10 = f32[8,128]{1,0:T(8,128)S(1)} collective-permute-done((f32[8,128]{1,0:T(8,128)S(1)}, f32[8,128]{1,0:T(8,128)S(1)}, u32[]{:S(2)}, u32[]{:S(2)}) %collective-permute-start.10) | collective-permute-done | bytes 4128 | tf_op jit(solution)/shard_map/ppermute | solution.py:562
  78.4 0.0 collective-permute-start.11
  78.4 3.6 %collective-permute-done.11 = f32[8,128]{1,0:T(8,128)S(1)} collective-permute-done((f32[8,128]{1,0:T(8,128)S(1)}, f32[8,128]{1,0:T(8,128)S(1)}, u32[]{:S(2)}, u32[]{:S(2)}) %collective-permute-start.11) | collective-permute-done | bytes 4128 | tf_op jit(solution)/shard_map/ppermute | solution.py:562
  82.0 0.2 collective-permute-start.12
  82.2 4.3 %collective-permute-done.12 = f32[8,128]{1,0:T(8,128)S(1)} collective-permute-done((f32[8,128]{1,0:T(8,128)S(1)}, f32[8,128]{1,0:T(8,128)S(1)}, u32[]{:S(2)}, u32[]{:S(2)}) %collective-permute-start.12) | collective-permute-done | bytes 4128 | tf_op jit(solution)/shard_map/ppermute | solution.py:562
  86.5 0.8 normalize.1
  (5 shorter events, 0.0 us)
Async XLA Ops:
  0.6 2.0 %copy-start.1 = (f32[27,32,1024]{2,1,0:T(8,128)S(1)}, f32[27,32,1024]{2,1,0:T(8,128)}, u32[]{:S(2)}) copy-start(f32[27,32,1024]{2,1,0:T(8,128)} %pops.1) | copy-start | bytes 10616836
  2.6 0.9 %copy-start.2 = (f32[32,1024]{1,0:T(8,128)S(1)}, f32[32,1024]{1,0:T(8,128)}, u32[]{:S(2)}) copy-start(f32[32,1024]{1,0:T(8,128)} %porosity.1) | copy-start | bytes 393220
  3.5 0.9 %copy-start.3 = (s32[32,1024]{1,0:T(8,128)S(1)}, s32[32,1024]{1,0:T(8,128)}, u32[]{:S(2)}) copy-start(s32[32,1024]{1,0:T(8,128)} %solid.1) | copy-start | bytes 393220
  4.4 0.9 %copy-start.4 = (s32[32,1024]{1,0:T(8,128)S(1)}, s32[32,1024]{1,0:T(8,128)}, u32[]{:S(2)}) copy-start(s32[32,1024]{1,0:T(8,128)} %labels.1) | copy-start | bytes 393220
  7.9 6.4 %collective-permute-start = (f32[240,128]{1,0:T(8,128)S(1)}, f32[240,128]{1,0:T(8,128)S(1)}, u32[]{:S(2)}, u32[]{:S(2)}) collective-permute-start(f32[240,128]{1,0:T(8,128)S(1)} %get-tuple-element.25), channel_id=1, source_target_pairs={{0,8},{8,0},{16,24},{24,16},{1,9},{9,1},{17,25},{25,17},{2,10},{10... | collective-permute-start | bytes 368648 | tf_op jit(solution)/shard_map/ppermute | solution.py:553
  11.0 8.2 %collective-permute-start.1 = (f32[240,128]{1,0:T(8,128)S(1)}, f32[240,128]{1,0:T(8,128)S(1)}, u32[]{:S(2)}, u32[]{:S(2)}) collective-permute-start(f32[240,128]{1,0:T(8,128)S(1)} %get-tuple-element.26), channel_id=1, source_target_pairs={{8,16},{16,8},{24,0},{0,24},{9,17},{17,9},{25,1},{1,25},{10,18},{1... | collective-permute-start | bytes 368648 | tf_op jit(solution)/shard_map/ppermute | solution.py:554
  19.2 15.4 %copy-start = (f32[27,32,1024]{2,1,0:T(8,128)S(1)}, f32[27,32,1024]{2,1,0:T(8,128)}, u32[]{:S(2)}) copy-start(f32[27,32,1024]{2,1,0:T(8,128)} %adjoint.1) | copy-start | bytes 10616836
  19.5 2.6 %collective-permute-start.2 = (f32[512,128]{1,0:T(8,128)S(1)}, f32[512,128]{1,0:T(8,128)S(1)}, u32[]{:S(2)}, u32[]{:S(2)}) collective-permute-start(f32[512,128]{1,0:T(8,128)S(1)} %get-tuple-element.28), channel_id=1, source_target_pairs={{0,1},{1,0},{2,3},{3,2},{4,5},{5,4},{6,7},{7,6},{8,9},{9,8},{10,11... | collective-permute-start | bytes 786440 | tf_op jit(solution)/shard_map/ppermute | solution.py:553
  19.6 9.0 %collective-permute-start.3 = (f32[512,128]{1,0:T(8,128)S(1)}, f32[512,128]{1,0:T(8,128)S(1)}, u32[]{:S(2)}, u32[]{:S(2)}) collective-permute-start(f32[512,128]{1,0:T(8,128)S(1)} %get-tuple-element.29), channel_id=1, source_target_pairs={{1,2},{2,1},{3,4},{4,3},{5,6},{6,5},{7,0},{0,7},{9,10},{10,9},{11,... | collective-permute-start | bytes 786440 | tf_op jit(solution)/shard_map/ppermute | solution.py:554
  40.7 5.1 %collective-permute-start.4 = (f32[216,128]{1,0:T(8,128)S(1)}, f32[216,128]{1,0:T(8,128)S(1)}, u32[]{:S(2)}, u32[]{:S(2)}) collective-permute-start(f32[216,128]{1,0:T(8,128)S(1)} %get-tuple-element.33), channel_id=1, source_target_pairs={{0,8},{8,0},{16,24},{24,16},{1,9},{9,1},{17,25},{25,17},{2,10},{10... | collective-permute-start | bytes 331784 | tf_op jit(solution)/shard_map/ppermute | solution.py:553
  41.3 8.1 %collective-permute-start.5 = (f32[216,128]{1,0:T(8,128)S(1)}, f32[216,128]{1,0:T(8,128)S(1)}, u32[]{:S(2)}, u32[]{:S(2)}) collective-permute-start(f32[216,128]{1,0:T(8,128)S(1)} %get-tuple-element.34), channel_id=1, source_target_pairs={{8,16},{16,8},{24,0},{0,24},{9,17},{17,9},{25,1},{1,25},{10,18},{1... | collective-permute-start | bytes 331784 | tf_op jit(solution)/shard_map/ppermute | solution.py:554
  49.6 2.0 %collective-permute-start.6 = (f32[480,128]{1,0:T(8,128)S(1)}, f32[480,128]{1,0:T(8,128)S(1)}, u32[]{:S(2)}, u32[]{:S(2)}) collective-permute-start(f32[480,128]{1,0:T(8,128)S(1)} %get-tuple-element.37), channel_id=1, source_target_pairs={{0,1},{1,0},{2,3},{3,2},{4,5},{5,4},{6,7},{7,6},{8,9},{9,8},{10,11... | collective-permute-start | bytes 737288 | tf_op jit(solution)/shard_map/ppermute | solution.py:553
  49.7 8.8 %collective-permute-start.7 = (f32[480,128]{1,0:T(8,128)S(1)}, f32[480,128]{1,0:T(8,128)S(1)}, u32[]{:S(2)}, u32[]{:S(2)}) collective-permute-start(f32[480,128]{1,0:T(8,128)S(1)} %get-tuple-element.38), channel_id=1, source_target_pairs={{1,2},{2,1},{3,4},{4,3},{5,6},{6,5},{7,0},{0,7},{9,10},{10,9},{11,... | collective-permute-start | bytes 737288 | tf_op jit(solution)/shard_map/ppermute | solution.py:554
  69.9 1.2 %collective-permute-start.8 = (f32[8,128]{1,0:T(8,128)S(1)}, f32[8,128]{1,0:T(8,128)S(1)}, u32[]{:S(2)}, u32[]{:S(2)}) collective-permute-start(f32[8,128]{1,0:T(8,128)S(1)} %get-tuple-element.44), channel_id=1, source_target_pairs={{0,1},{1,0},{2,3},{3,2},{4,5},{5,4},{6,7},{7,6},{8,9},{9,8},{10,11... | collective-permute-start | bytes 12296 | tf_op jit(solution)/shard_map/ppermute | solution.py:562
  71.1 3.6 %collective-permute-start.9 = (f32[8,128]{1,0:T(8,128)S(1)}, f32[8,128]{1,0:T(8,128)S(1)}, u32[]{:S(2)}, u32[]{:S(2)}) collective-permute-start(f32[8,128]{1,0:T(8,128)S(1)} %max.15), channel_id=1, source_target_pairs={{0,2},{1,3},{2,0},{3,1},{4,6},{5,7},{6,4},{7,5},{8,10},{9,11},{10,... | collective-permute-start | bytes 12296 | tf_op jit(solution)/shard_map/ppermute | solution.py:562
  74.7 3.6 %collective-permute-start.10 = (f32[8,128]{1,0:T(8,128)S(1)}, f32[8,128]{1,0:T(8,128)S(1)}, u32[]{:S(2)}, u32[]{:S(2)}) collective-permute-start(f32[8,128]{1,0:T(8,128)S(1)} %max.16), channel_id=1, source_target_pairs={{0,4},{1,5},{2,6},{3,7},{4,0},{5,1},{6,2},{7,3},{8,12},{9,13},{10,... | collective-permute-start | bytes 12296 | tf_op jit(solution)/shard_map/ppermute | solution.py:562
  78.4 3.6 %collective-permute-start.11 = (f32[8,128]{1,0:T(8,128)S(1)}, f32[8,128]{1,0:T(8,128)S(1)}, u32[]{:S(2)}, u32[]{:S(2)}) collective-permute-start(f32[8,128]{1,0:T(8,128)S(1)} %max.17), channel_id=1, source_target_pairs={{0,8},{8,0},{16,24},{24,16},{1,9},{9,1},{17,25},{25,17},{2,10},{10... | collective-permute-start | bytes 12296 | tf_op jit(solution)/shard_map/ppermute | solution.py:562
  82.0 4.5 %collective-permute-start.12 = (f32[8,128]{1,0:T(8,128)S(1)}, f32[8,128]{1,0:T(8,128)S(1)}, u32[]{:S(2)}, u32[]{:S(2)}) collective-permute-start(f32[8,128]{1,0:T(8,128)S(1)} %max.18), channel_id=1, source_target_pairs={{0,16},{8,24},{16,0},{24,8},{1,17},{9,25},{17,1},{25,9},{2,18},{10... | collective-permute-start | bytes 12296 | tf_op jit(solution)/shard_map/ppermute | solution.py:562
